TPU v7x, 256 devices: a whole 4x4x8 slice. The times are simulated.
256 devices in a mesh: grp: 8 (over z_lo, core), dev: 32 (over x, z_hi, y).
Axes of the slice: x: 4, y: 4, z: 8 (z_hi: 2, z_lo: 4; z = z_hi * 4 + z_lo), core: 2. Of those that a mesh axis runs over, the one named last changes fastest.
Arguments:
- density: float32 [2, 8192, 8192], P(None, 'dev', 'grp'), may hold values from -64 to 64, as said below
- costate: float32 [2, 8192, 8192], P(None, 'dev', 'grp'), may hold values from -64 to 64, as said below
- phases: float32 [24, 2, 64], replicated, may hold values from -3.140625 to 3.140625
- displacements: float32 [24, 2, 2, 64, 64], replicated, may hold values from -0.5 to 0.5
- table_slot: int32 [24], replicated, may hold values from 0 to 23, each once
- checkpoint: int32 [1], replicated, may hold values from 0 to 22
Outputs:
- costate_start: float32 [2, 8192, 8192], P(None, 'dev', 'grp')
- phase_grads: float32 [2, 2, 64], replicated
Inputs may be any that keep to these rules, and one draw needn't show every extreme that they name: `density`: Hermitian: real part symmetric, imaginary part antisymmetric. `costate`: Hermitian: real part symmetric, imaginary part antisymmetric. `table_slot`: every row of phases once.
All inputs are finite; a program needn't handle non-finite values.
Results may differ from a plain program's by a relative error of at most 0.00011.
Values sent between devices are 32-bit elements; how exact they have to be, the bound alone decides.
A program may use at most 128 MiB of HBM per device.

v0:
```python
import jax
import jax.numpy as jnp
from jax import lax
from jax.sharding import PartitionSpec as P

LEVELS = 64
TRANSMON = 2


HIGH = lax.Precision.HIGHEST


def quad(real_part, imag_part):
    return jnp.stack([jnp.stack([real_part, -imag_part]), jnp.stack([imag_part, real_part])])


def mode_apply(quads, field, dim):
    letters = "abcd"
    source = "p" + letters[: dim - 1] + "m" + letters[dim:]
    target = "o" + letters[: dim - 1] + "n" + letters[dim:]
    return jnp.einsum("opnm," + source + "->" + target, quads, field, precision=HIGH)


def turn(field, rows_angle, cols_angle):
    angles = rows_angle[:, :, None, None] - cols_angle[None, None, :, :]
    cosine = jnp.cos(angles)
    sine = jnp.sin(angles)
    return jnp.stack([cosine * field[0] - sine * field[1], sine * field[0] + cosine * field[1]])


def both_sides(field, real_part, imag_part, row_dim, forward):
    if forward:
        left_side = quad(real_part, imag_part)
        right_side = quad(real_part, -imag_part)
    else:
        left_side = quad(real_part.T, -imag_part.T)
        right_side = quad(real_part.T, imag_part.T)
    return mode_apply(right_side, mode_apply(left_side, field, row_dim), row_dim + 2)


def apply_first(field, matrix, forward):
    return both_sides(field, matrix[0], matrix[1], 1, forward)


def apply_second(field, matrix, forward):
    eye_block = jnp.eye(TRANSMON, dtype=jnp.float32)
    return both_sides(
        field, jnp.kron(matrix[0], eye_block), jnp.kron(matrix[1], eye_block), 2, forward
    )


def grad_terms(snapped, pulled):
    terms = 2.0 * jnp.sum(snapped[0] * pulled[1] - snapped[1] * pulled[0], axis=(2, 3))
    return jnp.sum(terms.reshape(terms.shape[0], terms.shape[1] // TRANSMON, TRANSMON), axis=2)


def angle_grid(table, first_start, first_count, second_start, second_count):
    first_part = lax.dynamic_slice_in_dim(table[0], first_start, first_count)
    second_part = lax.dynamic_slice_in_dim(table[1], second_start, second_count)
    grid = first_part[:, None] + second_part[None, :]
    return jnp.repeat(grid, TRANSMON, axis=1)


def place_part(values, offset, total):
    return lax.dynamic_update_slice_in_dim(jnp.zeros((total,), jnp.float32), values, offset, 0)


def toward_first(field):
    moved = lax.all_to_all(field, "dev", split_axis=2, concat_axis=1, tiled=True)
    return lax.all_to_all(moved, "grp", split_axis=4, concat_axis=3, tiled=True)


def toward_second(field):
    moved = lax.all_to_all(field, "dev", split_axis=1, concat_axis=2, tiled=True)
    return lax.all_to_all(moved, "grp", split_axis=3, concat_axis=4, tiled=True)


def layer_total(partial_value):
    return lax.psum(partial_value, ("grp", "dev"))


def per_device(density, costate, phases, displacements, table_slot, checkpoint):
    levels = LEVELS
    row_part = levels // lax.axis_size("dev")
    col_part = levels // lax.axis_size("grp")
    row_first = lax.axis_index("dev") * row_part
    col_first = lax.axis_index("grp") * col_part
    native = (2, row_part, levels * TRANSMON, col_part, levels * TRANSMON)
    state_zero = density.reshape(native)
    adjoint_two = costate.reshape(native)
    start = checkpoint[0]
    tables = []
    matrices = []
    for layer in range(2):
        slot = table_slot[start + layer]
        tables.append(lax.dynamic_index_in_dim(phases, slot, 0, keepdims=False))
        matrices.append(lax.dynamic_index_in_dim(displacements, start + layer, 0, keepdims=False))
    rows_zero = angle_grid(tables[0], row_first, row_part, 0, levels)
    cols_zero = angle_grid(tables[0], col_first, col_part, 0, levels)
    rows_one = angle_grid(tables[1], 0, levels, row_first, row_part)
    cols_one = angle_grid(tables[1], 0, levels, col_first, col_part)
    snapped_zero = turn(state_zero, rows_zero, cols_zero)
    moved = toward_first(apply_second(snapped_zero, matrices[0][1], True))
    state_one = apply_first(moved, matrices[0][0], True)
    snapped_one = turn(state_one, rows_one, cols_one)
    pulled = toward_first(apply_second(adjoint_two, matrices[1][1], False))
    pulled_one = apply_first(pulled, matrices[1][0], False)
    terms_one = grad_terms(snapped_one, pulled_one)
    partial_one = jnp.stack(
        [jnp.sum(terms_one, axis=1), place_part(jnp.sum(terms_one, axis=0), row_first, levels)]
    )
    total_one = layer_total(partial_one)
    adjoint_one = turn(pulled_one, -rows_one, -cols_one)
    returned = toward_second(apply_first(adjoint_one, matrices[0][0], False))
    pulled_zero = apply_second(returned, matrices[0][1], False)
    terms_zero = grad_terms(snapped_zero, pulled_zero)
    partial_zero = jnp.stack(
        [place_part(jnp.sum(terms_zero, axis=1), row_first, levels), jnp.sum(terms_zero, axis=0)]
    )
    adjoint_zero = turn(pulled_zero, -rows_zero, -cols_zero)
    gradients = jnp.stack([layer_total(partial_zero), total_one])
    return (adjoint_zero.reshape(costate.shape), gradients)


def solution(mesh):
    return jax.shard_map(
        per_device,
        mesh=mesh,
        in_specs=(P(None, "dev", "grp"), P(None, "dev", "grp"), P(), P(), P(), P()),
        out_specs=(P(None, "dev", "grp"), P()),
        check_vma=False,
    )
```

profile of v0, /device:TPU:1, one launch (start us, length us, event | category | flops | bytes accessed | tf_op | source)
XLA Modules:
  0.0 500.4 jit_solution(4917826877378254987)
XLA Ops:
  2.2 6.5 %broadcast_multiply_fusion = (f32[64,2,64,2]{3,2,1,0:T(8,128)}, f32[64,2,64,2]{3,2,1,0:T(8,128)}, f32[64,2,64,2]{3,2,1,0:T(8,128)}, f32[64,2,64,2]{3,2,1,0:T(8,128)}) fusion(f32[64,64]{1,0:T(8,128)S(1)} %get-tuple-element.24, f32[2,2]{1,0:T(2,128)S(1)} %compare_convert_fusion, f32[64,64]{1,0:T(8,128)S(1)} %get-tuple-element.31, ...), kind=kLoop, calls=%fused_computation.53 | loop fusion | flops 65536 | bytes 327696 | tf_op jit(solution)/shard_map/jit(kron)/mul | solution.py:48
  23.3 51.5 %all_to_all.108 = f32[2,2,128,8,128]{4,0,3,1,2:T(2,128)S(1)} all-to-all(f32[2,2,128,8,128]{4,0,3,1,2:T(2,128)S(1)} %copy.325), channel_id=1, replica_groups=mesh['grp'=8,'dev'=32] {'dev'}, dimensions={2} | all-to-all | bytes 4194304 | tf_op jit(solution)/shard_map/all_to_all | solution.py:69
  79.6 7.2 %reshape.330 = f32[8,1,65536]{2,1,0:T(1,128)} reshape(f32[128,2,4,8,64]{4,3,2,1,0:T(8,128)} %bitcast.413) | data formatting | bytes 4194304
  86.9 21.7 %all-to-all-start.1 = ((f32[8,1,65536]{2,1,0:T(1,128)}), f32[8,1,65536]{2,1,0:T(1,128)}, u32[]{:S(2)}, u32[]{:S(2)}) async-start(f32[8,1,65536]{2,1,0:T(1,128)} %reshape.330), calls=%async_computation.1 | async-start | bytes 4194304 | tf_op jit(solution)/shard_map/all_to_all | solution.py:70
  124.6 6.5 %fusion.71 = (f32[1,2,128,8,128]{2,4,0,3,1:T(8,128)S(1)}, f32[1,2,128,8,128]{2,4,0,3,1:T(8,128)S(1)}) fusion(f32[1,2,128,8,128]{2,4,0,3,1:T(8,128)} %copy.359, f32[1,2,128,8,128]{2,4,0,3,1:T(8,128)S(1)} %copy.358, f32[8,128]{1,0:T(8,128)S(1)} %copy.352, f32[2,128]{1,0:T(2,128)S(1)} %reshape.289), kind=kLoop, calls=%fused_computation.78 | loop fusion | flops 1835008 | bytes 4199424 | tf_op jit(solution)/shard_map/sub | solution.py:28
  139.5 17.2 %all-to-all-done.1 = f32[8,1,65536]{2,1,0:T(1,128)} async-done(((f32[8,1,65536]{2,1,0:T(1,128)}), f32[8,1,65536]{2,1,0:T(1,128)}, u32[]{:S(2)}, u32[]{:S(2)}) %all-to-all-start.1) | async-done | bytes 2097184 | tf_op jit(solution)/shard_map/all_to_all | solution.py:70
  156.8 5.0 all-to-all-start.4
  163.0 8.5 %reduce.10 = f32[8,65536]{1,0:T(8,128)} reduce(f32[8,1,65536]{2,1,0:T(1,128)} %all-to-all-done.1, f32[]{:T(128)} %broadcast.95), dimensions={1}, to_apply=%all_to_all.82.reduce_sub_computation | reduce | bytes 4194308 | tf_op jit(solution)/shard_map/all_to_all | solution.py:70
  171.6 5.2 %reshape.331 = f32[128,2,4,8,64]{4,3,2,1,0:T(8,128)} reshape(f32[8,65536]{1,0:T(8,128)} %reduce.10) | data formatting | bytes 4194304
  181.4 7.8 %fusion.10 = f32[2,64,4,64,16,1]{3,1,5,0,4,2:T(8,128)S(1)} fusion(f32[2,64,4,64,16,1]{1,4,3,2,0,5:T(8,128)S(1)} %bitcast.415, f32[1,2,64,64]{3,2,1,0:T(8,128)S(1)} %get-tuple-element.63, f32[1,2,64,64]{3,2,1,0:T(8,128)S(1)} %get-tuple-element.72), kind=kOutput, calls=%fused_computation.11 | convolution fusion | flops 805322752 | bytes 4259840 | tf_op jit(solution)/shard_map/opnm,pmbcd->onbcd/dot_general | solution.py:21
  189.1 6.6 %fusion.23 = f32[2,64,4,64,16]{1,3,0,4,2:T(8,128)S(1)} fusion(f32[2,64,4,64,16,1]{3,1,5,0,4,2:T(8,128)S(1)} %fusion.10, f32[1,2,64,64]{3,2,1,0:T(8,128)S(1)} %get-tuple-element.73, f32[1,2,64,64]{3,2,1,0:T(8,128)S(1)} %get-tuple-element.62), kind=kOutput, calls=%fused_computation.26 | convolution fusion | flops 805322752 | bytes 4259840 | tf_op jit(solution)/shard_map/opnm,pabmd->oabnd/dot_general | solution.py:21
  195.8 8.2 %fusion.35 = (f32[1,64,4,64,16]{1,3,4,2,0:T(8,128)S(1)}, f32[1,64,4,64,16]{1,3,4,2,0:T(8,128)S(1)}) fusion(f32[2,64,4,64,16]{1,3,0,4,2:T(8,128)S(1)} %fusion.23, f32[64,16]{0,1:T(8,128)S(1)} %neg.76, f32[64,4]{0,1:T(4,128)S(1)} %neg.75), kind=kLoop, calls=%fused_computation.34 | loop fusion | flops 1835008 | bytes 4199424 | tf_op jit(solution)/shard_map/sub | solution.py:28
  204.0 6.6 %fusion.8 = f32[2,64,4,64,16,1]{3,1,5,0,4,2:T(8,128)S(1)} fusion(f32[1,2,64,64]{3,2,1,0:T(8,128)S(1)} %get-tuple-element.59, f32[1,2,64,64]{3,2,1,0:T(8,128)S(1)} %get-tuple-element.70, f32[1,64,4,64,16]{1,3,4,2,0:T(8,128)S(1)} %get-tuple-element.23, f32[1,64,4,64,16]{1,3,4,2,0:T(8,128)S(1)} %get-tuple-element.22), kind=kOutput, calls=%fused_computation.9 | convolution fusion | flops 805847040 | bytes 4259840 | tf_op jit(solution)/shard_map/opnm,pmbcd->onbcd/dot_general | solution.py:21
  214.3 5.6 %copy.462 = f32[2,64,4,64,16]{3,0,4,2,1:T(2,128)} copy(f32[2,64,4,64,16]{3,1,0,4,2:T(8,128)S(1)} %fusion.26) | data formatting | bytes 4194304 | tf_op jit(solution)/shard_map/opnm,pabmd->oabnd/transpose | solution.py:21
  219.9 6.6 %reshape.332 = f32[32,1,16384]{2,1,0:T(1,128)} reshape(f32[64,4,16,2,64]{4,3,2,1,0:T(2,128)} %bitcast.418) | data formatting | bytes 4194304
  226.5 11.7 %all-to-all-start.2 = ((f32[32,1,16384]{2,1,0:T(1,128)}), f32[32,1,16384]{2,1,0:T(1,128)}, u32[]{:S(2)}, u32[]{:S(2)}) async-start(f32[32,1,16384]{2,1,0:T(1,128)} %reshape.332), calls=%async_computation.2 | async-start | bytes 4194304 | tf_op jit(solution)/shard_map/all_to_all | solution.py:74
  241.5 5.6 %copy.366 = f32[2,64,4,8,128]{1,3,2,0,4:T(8,128)} copy(f32[2,64,4,8,128]{4,3,2,1,0:T(8,128)} %bitcast.427) | data formatting | bytes 4194304 | tf_op jit(solution)/shard_map/all_to_all | solution.py:69
  247.0 7.2 %reshape.334 = f32[8,1,65536]{2,1,0:T(1,128)} reshape(f32[128,2,4,8,64]{4,3,2,1,0:T(8,128)} %bitcast.414) | data formatting | bytes 4194304
  254.3 34.7 %all-to-all-done.2 = f32[32,1,16384]{2,1,0:T(1,128)} async-done(((f32[32,1,16384]{2,1,0:T(1,128)}), f32[32,1,16384]{2,1,0:T(1,128)}, u32[]{:S(2)}, u32[]{:S(2)}) %all-to-all-start.2) | async-done | bytes 2097184 | tf_op jit(solution)/shard_map/all_to_all | solution.py:74
  289.0 6.4 %all-to-all-start.5 = ((f32[8,1,65536]{2,1,0:T(1,128)}), f32[8,1,65536]{2,1,0:T(1,128)}, u32[]{:S(2)}, u32[]{:S(2)}) async-start(f32[8,1,65536]{2,1,0:T(1,128)} %reshape.334), calls=%async_computation.5 | async-start | bytes 4194304 | tf_op jit(solution)/shard_map/all_to_all | solution.py:70
  295.4 8.7 %reduce.11 = f32[32,16384]{1,0:T(8,128)} reduce(f32[32,1,16384]{2,1,0:T(1,128)} %all-to-all-done.2, f32[]{:T(128)} %broadcast.95), dimensions={1}, to_apply=%all_to_all.86.reduce_sub_computation | reduce | bytes 4194308 | tf_op jit(solution)/shard_map/all_to_all | solution.py:74
  304.2 5.6 %reshape.333 = f32[64,4,16,2,64]{4,3,2,1,0:T(2,128)} reshape(f32[32,16384]{1,0:T(8,128)} %reduce.11) | data formatting | bytes 4194304
  314.5 4.9 copy.338
  319.3 24.4 %all-to-all-done.5 = f32[8,1,65536]{2,1,0:T(1,128)} async-done(((f32[8,1,65536]{2,1,0:T(1,128)}), f32[8,1,65536]{2,1,0:T(1,128)}, u32[]{:S(2)}, u32[]{:S(2)}) %all-to-all-start.5) | async-done | bytes 2097184 | tf_op jit(solution)/shard_map/all_to_all | solution.py:70
  343.8 5.1 %all-to-all-start.3 = ((f32[2,2,128,64,16]{2,4,1,0,3:T(8,128)}), f32[2,2,128,64,16]{2,4,1,0,3:T(8,128)}, u32[]{:S(2)}, u32[]{:S(2)}) async-start(f32[2,2,128,64,16]{2,4,1,0,3:T(8,128)} %copy.338), calls=%async_computation.3 | async-start | bytes 4194304 | tf_op jit(solution)/shard_map/all_to_all | solution.py:75
  361.2 7.2 %reduce.12 = f32[8,65536]{1,0:T(8,128)S(1)} reduce(f32[8,1,65536]{2,1,0:T(1,128)} %all-to-all-done.5, f32[]{:T(128)} %broadcast.95), dimensions={1}, to_apply=%all_to_all.98.reduce_sub_computation | reduce | bytes 4194308 | tf_op jit(solution)/shard_map/all_to_all | solution.py:70
  376.8 8.2 %fusion.6 = f32[2,64,4,64,16,1]{3,1,5,0,4,2:T(8,128)S(1)} fusion(f32[2,64,4,64,16,1]{1,4,3,2,0,5:T(8,128)S(1)} %bitcast.416, f32[1,2,64,64]{2,3,1,0:T(8,128)S(1)} %copy-done.9, f32[1,2,64,64]{2,3,1,0:T(8,128)S(1)} %copy-done.10), kind=kOutput, calls=%fused_computation.7 | convolution fusion | flops 805322752 | bytes 4259840 | tf_op jit(solution)/shard_map/opnm,pmbcd->onbcd/dot_general | solution.py:21
  385.1 6.8 %fusion.20 = f32[2,64,4,64,16]{1,3,4,2,0:T(8,128)S(1)} fusion(f32[2,64,4,64,16,1]{3,1,5,0,4,2:T(8,128)S(1)} %fusion.6, f32[1,2,64,64]{2,3,1,0:T(8,128)S(1)} %copy-done.8, f32[1,2,64,64]{2,3,1,0:T(8,128)S(1)} %copy-done.7), kind=kOutput, calls=%fused_computation.25 | convolution fusion | flops 805322752 | bytes 4259840 | tf_op jit(solution)/shard_map/opnm,pabmd->oabnd/dot_general | solution.py:21
  391.9 9.2 %fusion.32 = f32[64,4]{0,1:T(4,128)S(1)} fusion(f32[2,64,4,64,16]{1,3,4,2,0:T(8,128)S(1)} %fusion.20, f32[2,64,4,64,16]{1,3,0,4,2:T(8,128)S(1)} %copy-done.1, f32[64,16]{0,1:T(8,128)S(1)} %bitcast.448, f32[64,4]{0,1:T(4,128)S(1)} %bitcast.450), kind=kLoop, calls=%fused_computation.31 | loop fusion | flops 2883328 | bytes 4200448 | tf_op jit(solution)/shard_map/reduce_sum | solution.py:53
  407.4 4.8 fusion.76
  412.5 5.5 %fusion.79 = (f32[1,2,128,8,128]{2,4,3,1,0:T(8,128)}, f32[1,2,128,8,128]{2,4,3,1,0:T(8,128)S(1)}) fusion(f32[2,2,128,8,128]{2,4,0,3,1:T(8,128)S(1)} %fusion.53, f32[8,128]{1,0:T(8,128)S(1)} %copy.317, f32[2,128]{1,0:T(2,128)S(1)} %neg.72), kind=kLoop, calls=%fused_computation.86 | loop fusion | flops 1835008 | bytes 4199424 | tf_op jit(solution)/shard_map/sub | solution.py:28
  424.1 75.3 %all-reduce = (f32[1,2,64]{2,1,0:T(2,128)S(1)}, f32[1,2,64]{2,1,0:T(2,128)S(1)}) all-reduce(f32[1,2,64]{2,1,0:T(2,128)S(1)} %maximum_bitcast_fusion.28, f32[1,2,64]{2,1,0:T(2,128)S(1)} %maximum_bitcast_fusion.27), channel_id=1, replica_groups=mesh['grp'=8,'dev'=32] {'grp','dev'}, use_global_device_ids=true, to_apply=%region_9.10 | all-reduce | flops 256 | bytes 2048 | tf_op jit(solution)/shard_map/psum | solution.py:79
  (123 shorter events, 92.3 us)
Async XLA Ops:
  12.8 4.3 copy-start.3
  86.8 21.7 %copy-start.12 = (s32[24]{0:T(128)S(1)}, s32[24]{0:T(128)}, u32[]{:S(2)}) copy-start(s32[24]{0:T(128)} %param.10) | copy-start | bytes 292
  86.9 27.2 %copy-start.4 = (f32[2,256,1024]{2,1,0:T(8,128)S(1)}, f32[2,256,1024]{2,1,0:T(8,128)}, u32[]{:S(2)}) copy-start(f32[2,256,1024]{2,1,0:T(8,128)} %param.6) | copy-start | bytes 6291460
  86.9 69.9 %all-to-all-start.1 = ((f32[8,1,65536]{2,1,0:T(1,128)}), f32[8,1,65536]{2,1,0:T(1,128)}, u32[]{:S(2)}, u32[]{:S(2)}) async-start(f32[8,1,65536]{2,1,0:T(1,128)} %reshape.330), calls=%async_computation.1 | async-start | bytes 4194304 | tf_op jit(solution)/shard_map/all_to_all | solution.py:70
  156.8 69.7 %all-to-all-start.4 = ((f32[2,2,128,8,128]{4,0,3,1,2:T(2,128)}), f32[2,2,128,8,128]{4,0,3,1,2:T(2,128)}, u32[]{:S(2)}, u32[]{:S(2)}) async-start(f32[2,2,128,8,128]{4,0,3,1,2:T(2,128)} %copy.363), calls=%async_computation.4 | async-start | bytes 4194304 | tf_op jit(solution)/shard_map/all_to_all | solution.py:69
  195.8 8.2 %copy-start = (f32[2,64,4,64,16]{1,3,0,4,2:T(8,128)}, f32[2,64,4,64,16]{1,3,0,4,2:T(8,128)S(1)}, u32[]{:S(2)}) copy-start(f32[2,64,4,64,16]{1,3,0,4,2:T(8,128)S(1)} %fusion.23) | copy-start | bytes 6291460
  226.5 62.5 %all-to-all-start.2 = ((f32[32,1,16384]{2,1,0:T(1,128)}), f32[32,1,16384]{2,1,0:T(1,128)}, u32[]{:S(2)}, u32[]{:S(2)}) async-start(f32[32,1,16384]{2,1,0:T(1,128)} %reshape.332), calls=%async_computation.2 | async-start | bytes 4194304 | tf_op jit(solution)/shard_map/all_to_all | solution.py:74
  289.0 54.8 %all-to-all-start.5 = ((f32[8,1,65536]{2,1,0:T(1,128)}), f32[8,1,65536]{2,1,0:T(1,128)}, u32[]{:S(2)}, u32[]{:S(2)}) async-start(f32[8,1,65536]{2,1,0:T(1,128)} %reshape.334), calls=%async_computation.5 | async-start | bytes 4194304 | tf_op jit(solution)/shard_map/all_to_all | solution.py:70
  343.8 57.8 %all-to-all-start.3 = ((f32[2,2,128,64,16]{2,4,1,0,3:T(8,128)}), f32[2,2,128,64,16]{2,4,1,0,3:T(8,128)}, u32[]{:S(2)}, u32[]{:S(2)}) async-start(f32[2,2,128,64,16]{2,4,1,0,3:T(8,128)} %copy.338), calls=%async_computation.3 | async-start | bytes 4194304 | tf_op jit(solution)/shard_map/all_to_all | solution.py:75
  358.3 2.2 copy-start.11
  372.1 4.7 copy-start.9
  372.1 4.7 copy-start.10
  376.8 8.3 %copy-start.7 = (f32[1,2,64,64]{2,3,1,0:T(8,128)S(1)}, f32[1,2,64,64]{2,3,1,0:T(8,128)}, u32[]{:S(2)}) copy-start(f32[1,2,64,64]{2,3,1,0:T(8,128)} %get-tuple-element.50) | copy-start | bytes 98308
  376.8 8.3 %copy-start.8 = (f32[1,2,64,64]{2,3,1,0:T(8,128)S(1)}, f32[1,2,64,64]{2,3,1,0:T(8,128)}, u32[]{:S(2)}) copy-start(f32[1,2,64,64]{2,3,1,0:T(8,128)} %get-tuple-element.69) | copy-start | bytes 98308
  385.1 6.8 %copy-start.1 = (f32[2,64,4,64,16]{1,3,0,4,2:T(8,128)S(1)}, f32[2,64,4,64,16]{1,3,0,4,2:T(8,128)}, u32[]{:S(2)}) copy-start(f32[2,64,4,64,16]{1,3,0,4,2:T(8,128)} %copy-done) | copy-start | bytes 6291460
  401.5 1.9 copy-start.5
  401.6 1.9 copy-start.6
  405.4 2.0 copy-start.2
where the time goes:
time: 511 us; the launch traced here: 500 us
  blocking collectives  127 us (25%)
  local copies, waits for them, and re-layouts  118 us (23%)
  waiting for transfers between devices  76.4 us (15%)
  other arithmetic  70.1 us (14%)
  matrix products  53.1 us (10%)
  starting transfers between devices  49.9 us (10%)
  between operations  6.02 us (1%)
    psum x1, blocking collectives, layer_total(): return lax.psum(partial_value, ('grp', 'dev'))  75.3 us
    dot_general x12, matrix products, mode_apply(): jnp.einsum('opnm,' + source + '->' + target, quads, field, precision=HIGH)  53.1 us
    all_to_all x1, blocking collectives, toward_first(): lax.all_to_all(field, 'dev', split_axis=2, concat_axis=1, tiled=True)  51.5 us
    all_to_all x2, waiting for transfers between devices, toward_first(): return lax.all_to_all(moved, 'grp', split_axis=4, concat_axis=3, tiled=True)  41.7 us
    unnamed x41, local copies, waits for them, and re-layouts  38.9 us
    all_to_all x1, waiting for transfers between devices, toward_second(): lax.all_to_all(field, 'dev', split_axis=1, concat_axis=2, tiled=True)  34.7 us
    all_to_all x2, starting transfers between devices, toward_first(): return lax.all_to_all(moved, 'grp', split_axis=4, concat_axis=3, tiled=True)  28.1 us
    sub x3, other arithmetic, turn(): cosine * field[0] - sine * field[1]  20.2 us
  transfers between devices with their start and end apart: 5, of which 3 were waited for; matrix products, arithmetic and copies ran while one was open for 37% of the time, Pallas kernels for 0%

commit v1 on v0

v1 whole, which is shorter than its diff:
```python
import functools

import jax
import jax.numpy as jnp
from jax import lax
from jax.experimental import pallas as pl
from jax.experimental.pallas import tpu as pltpu
from jax.sharding import PartitionSpec as P

LEVELS = 64
HIGH = lax.Precision.HIGH
HIGHEST = lax.Precision.HIGHEST


def place():
    g = lax.axis_index("grp")
    d = lax.axis_index("dev")
    return d // 8, (d // 4) % 2 * 4 + g // 2, d % 4, g % 2


def exchange_kernel(same, x_ref, o_ref, local_sem, send_sem, recv_sem):
    x, z, y, core = place()
    me = lax.axis_index("dev") * 8 + lax.axis_index("grp")
    own = pltpu.make_async_copy(x_ref.at[0] if same else x_ref.at[me], o_ref.at[me], local_sem)
    own.start()

    def body(step, carry):
        s = (step * 37) % 256
        tz = (z + s % 8) % 8
        tx = (x + s // 8 % 4) % 4
        ty = (y + s // 32 % 4) % 4
        tc = (core + s // 128) % 2
        td = tx * 8 + tz // 4 * 4 + ty
        tg = tz % 4 * 2 + tc
        pltpu.make_async_remote_copy(
            src_ref=x_ref.at[0] if same else x_ref.at[td * 8 + tg],
            dst_ref=o_ref.at[me],
            send_sem=send_sem,
            recv_sem=recv_sem,
            device_id=(tg, td),
            device_id_type=pl.DeviceIdType.MESH,
        ).start()
        return carry

    lax.fori_loop(1, 256, body, 0)
    own.wait()
    rest = o_ref.at[pl.ds(0, 255)]
    pltpu.make_async_copy(rest, rest, send_sem).wait()
    pltpu.make_async_copy(rest, rest, recv_sem).wait()


def exchange(x, same=False):
    return pl.pallas_call(
        functools.partial(exchange_kernel, same),
        out_shape=jax.ShapeDtypeStruct((256,) + x.shape[1:], x.dtype),
        in_specs=[pl.BlockSpec(memory_space=pltpu.VMEM)],
        out_specs=pl.BlockSpec(memory_space=pltpu.VMEM),
        scratch_shapes=[pltpu.SemaphoreType.DMA] * 3,
        compiler_params=pltpu.CompilerParams(has_side_effects=True, vmem_limit_bytes=40 * 2**20),
    )(x)


def cmul(spec, a, b, precision=HIGHEST):
    dot = functools.partial(jnp.einsum, spec, precision=precision)
    return jnp.stack([dot(a[0], b[0]) - dot(a[1], b[1]), dot(a[0], b[1]) + dot(a[1], b[0])])


def conj(a):
    return jnp.stack([a[0], -a[1]])


def phase_columns(matrix, angle):
    return cmul("ij,j->ij", matrix, jnp.stack([jnp.cos(angle), jnp.sin(angle)]))


def there(field):
    f = field.reshape(2, 2, 16, 8, 8, 16, 8)
    f = f.transpose(2, 5, 0, 1, 4, 3, 6).reshape(256, 16, 128)
    f = exchange(f).reshape(32, 8, 2, 2, 8, 64)
    return f.transpose(2, 0, 3, 1, 4, 5).reshape(2, 64, 64, 64)


def back(field):
    f = field.reshape(2, 32, 2, 8, 8, 64)
    f = f.transpose(1, 3, 0, 2, 4, 5).reshape(256, 16, 128)
    f = exchange(f).reshape(16, 16, 2, 2, 8, 8, 8)
    return f.transpose(2, 3, 0, 5, 4, 1, 6).reshape(2, 2, 128, 8, 128)


def per_device(density, costate, phases, displacements, table_slot, checkpoint):
    start = checkpoint[0]
    table = [phases[table_slot[start + l]] for l in range(2)]
    disp = [displacements[start + l] for l in range(2)]
    va, wa = [phase_columns(disp[l][0], table[l][0]) for l in range(2)]
    vb, wb = [phase_columns(disp[l][1], table[l][1]) for l in range(2)]
    ua = cmul("ij,jk->ik", wa, va)
    ub = cmul("ij,jk->ik", wb, vb)
    eye = jnp.eye(2, dtype=jnp.float32)
    ub2 = jnp.stack([jnp.kron(ub[0], eye), jnp.kron(ub[1], eye)])

    rho = density.reshape(2, 2, 128, 8, 128)
    c = there(costate)
    r = cmul("ij,ajbk->aibk", ub2, rho, HIGH)
    r = cmul("aibk,jk->aibj", r, conj(ub2), HIGH)
    r = there(r)
    q = cmul("nap,ab->nbp", c, ua, HIGH)
    y = back(cmul("nc,nap->cap", conj(ua), q, HIGH))
    f = cmul("nap,bap->nb", q, conj(r), HIGH)
    t = cmul("aibj,jk->aibk", y, ub2, HIGH)
    out = cmul("ki,akbj->aibj", conj(ub2), t, HIGH)
    jj = cmul("aibk,ajbk->ij", t, conj(rho), HIGH)
    jj = jj.reshape(2, 64, 2, 64, 2)
    jj = jj[:, :, 0, :, 0] + jj[:, :, 1, :, 1]

    def diag(a, b):
        return 2.0 * cmul("ij,ji->i", a, b)[1]

    def dagger(a):
        return conj(a.transpose(0, 2, 1))

    def grads(u, v, w, m):
        first = diag(dagger(u), m)
        second = diag(dagger(w), cmul("ij,jk->ik", m, dagger(v)))
        return jnp.stack([first, second])

    parts = jnp.stack([grads(ua, va, wa, f), grads(ub, vb, wb, jj)], axis=1)
    total = jnp.sum(exchange(parts.reshape(1, 2, 128), same=True), axis=0).reshape(2, 2, 64)
    return out.reshape(2, 256, 1024), total


def solution(mesh):
    return jax.shard_map(
        per_device,
        mesh=mesh,
        in_specs=(P(None, "dev", "grp"), P(None, "dev", "grp"), P(), P(), P(), P()),
        out_specs=(P(None, "dev", "grp"), P()),
        check_vma=False,
    )
```

time: 511 us -> 571 us (1.12)
  Pallas kernels: 0 us -> 215 us
  local copies, waits for them, and re-layouts: 118 us -> 255 us
  blocking collectives: 127 us -> 0 us
  waiting for transfers between devices: 76.4 us -> 0 us
  starting transfers between devices: 49.9 us -> 0 us
  other arithmetic: 70.1 us -> 38 us
  matrix products: 53.1 us -> 45.9 us
    pallas_call x0 -> x4, Pallas kernels: none -> 215 us  [exchange(): pl.pallas_call(functools.partial(exchange_kernel, same), out_shape=jax.Sh...]
    all_to_all x5 -> x0, waiting for transfers between devices: 76.4 us -> none  [the longest x2 41.7 us: toward_first(): return lax.all_to_all(moved, 'grp', split_axis=4, concat_axis=3, tiled=True)]
    psum x1 -> x0, blocking collectives: 75.3 us -> none  [layer_total(): return lax.psum(partial_value, ('grp', 'dev'))]
    reshape x2 -> x11, local copies, waits for them, and re-layouts: 0.22 us -> 65.5 us  [the longest x4 26.7 us: there(): f = f.transpose(2, 5, 0, 1, 4, 3, 6).reshape(256, 16, 128)]
    all_to_all x1 -> x0, blocking collectives: 51.5 us -> none  [toward_first(): lax.all_to_all(field, 'dev', split_axis=2, concat_axis=1, tiled=True)]
    all_to_all x5 -> x0, starting transfers between devices: 49.9 us -> none  [the longest x2 28.1 us: toward_first(): return lax.all_to_all(moved, 'grp', split_axis=4, concat_axis=3, tiled=True)]
    squeeze x4, local copies, waits for them, and re-layouts: 3.5 us -> 48.2 us  [the longest x2 24.1 us: cmul(): a[1]]
    another operation x2 -> x11, local copies, waits for them, and re-layouts: 0.01 us -> 44.7 us  [the longest x10 44.7 us: cmul(): jnp.stack([dot(a[0], b[0]) - dot(a[1], b[1]), dot(a[0], b[1]) + dot(a[1],...]
  transfers between devices with their start and end apart: 5 -> 0, of which waited for: 3 -> 0; matrix products, arithmetic and copies ran while one was open for 37% -> 0% of each run, Pallas kernels for 0% -> 0%
where the time goes in v1:
time: 571 us; the launch traced here: 561 us
  local copies, waits for them, and re-layouts  255 us (45%)
  Pallas kernels  215 us (38%)
  matrix products  45.9 us (8%)
  other arithmetic  38 us (7%)
  between operations  6.63 us (1%)
    pallas_call x4, Pallas kernels, exchange(): pl.pallas_call(functools.partial(exchange_kernel, same), out_shape=jax.Sh...  215 us
    transpose x2, local copies, waits for them, and re-layouts, there(): f = f.transpose(2, 5, 0, 1, 4, 3, 6).reshape(256, 16, 128)  49.7 us
    another operation x10, local copies, waits for them, and re-layouts, cmul(): jnp.stack([dot(a[0], b[0]) - dot(a[1], b[1]), dot(a[0], b[1]) + dot(a[1],...  44.7 us
    reshape x4, local copies, waits for them, and re-layouts, there(): f = f.transpose(2, 5, 0, 1, 4, 3, 6).reshape(256, 16, 128)  26.7 us
    squeeze x2, local copies, waits for them, and re-layouts, cmul(): a[1]  24.1 us
    squeeze x2, local copies, waits for them, and re-layouts, cmul(): a[0]  24.1 us
    transpose x1, other arithmetic, there(): f = f.transpose(2, 5, 0, 1, 4, 3, 6).reshape(256, 16, 128)  23.3 us
    reshape x1, local copies, waits for them, and re-layouts, there(): f = field.reshape(2, 2, 16, 8, 8, 16, 8)  21.1 us

profile of v1, /device:TPU:1, one launch (start us, length us, event | category | flops | bytes accessed | tf_op | source)
XLA Modules:
  0.0 560.6 jit_solution(10789141380342237642)
XLA Ops:
  9.2 5.4 fusion.26
  14.6 4.0 reshape.205
  21.2 4.0 reshape.206
  29.2 4.1 reshape.207
  34.5 11.1 %stack.126 = f32[1,2,16,8,8,16,8]{6,5,4,3,2,1,0:T(8,128)} reshape(f32[2,128,8,128]{3,2,1,0:T(8,128)S(1)} %copy.124) | data formatting | bytes 2097152 | tf_op jit(solution)/shard_map/stack | solution.py:65
  47.4 11.3 %stack.127 = f32[1,2,16,8,8,16,8]{6,5,4,3,2,1,0:T(8,128)} reshape(f32[2,128,8,128]{3,2,1,0:T(8,128)S(1)} %copy.125) | data formatting | bytes 2097152 | tf_op jit(solution)/shard_map/stack | solution.py:65
  58.7 23.3 %maximum_bitcast_fusion = f32[16,16,2,2,8,8,8]{6,1,4,5,0,3,2:T(8,128)} fusion(f32[1,2,16,8,8,16,8]{6,5,4,3,2,1,0:T(8,128)} %stack.127, f32[1,2,16,8,8,16,8]{6,5,4,3,2,1,0:T(8,128)} %stack.126), kind=kLoop, calls=%fused_computation | loop fusion | flops 524288 | bytes 4194304 | tf_op jit(solution)/shard_map/transpose | solution.py:78
  82.0 24.8 %copy.126 = f32[16,16,2,2,8,8,8]{1,0,6,5,4,3,2:T(8,128)} copy(f32[16,16,2,2,8,8,8]{6,1,4,5,0,3,2:T(8,128)} %maximum_bitcast_fusion) | data formatting | bytes 4194304 | tf_op jit(solution)/shard_map/transpose | solution.py:78
  106.9 11.4 %reshape.193 = f32[256,16,128]{0,2,1:T(8,128)S(1)} reshape(f32[16,16,2,2,8,8,8]{1,0,6,5,4,3,2:T(8,128)} %copy.126) | data formatting | bytes 4194304 | tf_op jit(solution)/shard_map/reshape | solution.py:78
  121.8 68.6 %shard_map.79 = f32[256,16,128]{2,1,0:T(8,128)S(1)} custom-call(f32[256,16,128]{2,1,0:T(8,128)S(1)} %copy-done), custom_call_target="tpu_custom_call" | custom-call | tf_op jit(solution)/shard_map/pallas_call | solution.py:53
  192.8 4.0 slice_negate_fusion
  199.6 21.1 %reshape.188 = f32[2,2,16,8,8,16,8]{6,5,4,3,2,1,0:T(8,128)} reshape(f32[2,256,1024]{2,1,0:T(8,128)S(1)} %copy-done.19) | data formatting | bytes 4194304 | tf_op jit(solution)/shard_map/reshape | solution.py:77
  220.8 24.8 %copy.89 = f32[16,16,2,2,8,8,8]{1,0,6,5,4,3,2:T(8,128)} copy(f32[16,16,2,2,8,8,8]{6,1,4,5,0,3,2:T(8,128)} %bitcast.413) | data formatting | bytes 4194304 | tf_op jit(solution)/shard_map/transpose | solution.py:78
  245.6 11.4 %reshape.189 = f32[256,16,128]{0,2,1:T(8,128)S(1)} reshape(f32[16,16,2,2,8,8,8]{1,0,6,5,4,3,2:T(8,128)} %copy.89) | data formatting | bytes 4194304 | tf_op jit(solution)/shard_map/reshape | solution.py:78
  260.6 59.2 %shard_map.77 = f32[256,16,128]{2,1,0:T(8,128)S(1)} custom-call(f32[256,16,128]{2,1,0:T(8,128)S(1)} %copy-done.1), custom_call_target="tpu_custom_call" | custom-call | tf_op jit(solution)/shard_map/pallas_call | solution.py:53
  319.8 2.7 reshape.190
  322.5 2.6 fusion.137
  336.4 2.6 fusion.52
  356.1 3.3 reshape.191.x_ref
  359.3 59.4 %shard_map.78 = f32[256,16,128]{2,1,0:T(8,128)S(1)} custom-call(f32[256,16,128]{2,1,0:T(8,128)S(1)} %reshape.191.x_ref), custom_call_target="tpu_custom_call" | custom-call | tf_op jit(solution)/shard_map/pallas_call | solution.py:53
  422.0 8.6 %reshape.192 = f32[16,16,2,2,8,8,8]{1,0,6,5,4,3,2:T(8,128)} reshape(f32[256,16,128]{0,2,1:T(8,128)S(1)} %copy.107) | data formatting | bytes 4194304 | tf_op jit(solution)/shard_map/reshape | solution.py:86
  430.6 10.8 %fusion.136 = (f32[1,2,16,8,8,16,8]{5,2,6,3,4,1,0:T(8,128)}, f32[1,2,16,8,8,16,8]{5,2,6,3,4,1,0:T(8,128)}) fusion(f32[2,2,16,8,8,16,8]{5,2,6,3,4,1,0:T(8,128)} %bitcast.414), kind=kLoop, calls=%fused_computation.199 | loop fusion | bytes 4194304 | tf_op jit(solution)/shard_map/slice | solution.py:65
  441.4 12.3 %copy.207 = f32[1,2,16,8,8,16,8]{6,5,3,2,4,1,0:T(8,128)} copy(f32[1,2,16,8,8,16,8]{5,2,6,3,4,1,0:T(8,128)} %get-tuple-element.7) | data formatting | bytes 2097152 | tf_op jit(solution)/shard_map/squeeze | solution.py:65
  453.8 11.8 %reshape.243 = f32[2,128,8,128]{3,1,2,0:T(8,128)S(1)} reshape(f32[1,2,16,8,8,16,8]{6,5,3,2,4,1,0:T(8,128)} %copy.207) | data formatting | bytes 2097152 | tf_op jit(solution)/shard_map/squeeze | solution.py:65
  467.1 12.3 %copy.208 = f32[1,2,16,8,8,16,8]{6,5,3,2,4,1,0:T(8,128)} copy(f32[1,2,16,8,8,16,8]{5,2,6,3,4,1,0:T(8,128)} %get-tuple-element.6) | data formatting | bytes 2097152 | tf_op jit(solution)/shard_map/squeeze | solution.py:65
  479.5 11.8 %reshape.244 = f32[2,128,8,128]{3,1,2,0:T(8,128)S(1)} reshape(f32[1,2,16,8,8,16,8]{6,5,3,2,4,1,0:T(8,128)} %copy.208) | data formatting | bytes 2097152 | tf_op jit(solution)/shard_map/squeeze | solution.py:65
  498.6 5.5 stack.142
  504.1 3.0 copy.137
  509.1 5.8 %stack.143 = f32[1,64,2,64,2]{4,3,2,1,0:T(8,128)} reshape(f32[128,128]{1,0:T(8,128)S(1)} %fusion.28) | data formatting | bytes 131072 | tf_op jit(solution)/shard_map/stack | solution.py:65
  514.9 3.1 copy.138
  519.1 27.4 %shard_map.80 = f32[256,2,128]{2,1,0:T(2,128)S(1)} custom-call(f32[1,2,128]{2,1,0:T(2,128)S(1)} %reshape.195.x_ref), custom_call_target="tpu_custom_call" | custom-call | tf_op jit(solution)/shard_map/pallas_call | solution.py:53
  550.4 2.6 copy.116
  (163 shorter events, 79.8 us)
Async XLA Ops:
  8.8 5.8 %copy-start.32 = (f32[64,64]{1,0:T(8,128)}, f32[64,64]{1,0:T(8,128)S(1)}, u32[]{:S(2)}) copy-start(f32[64,64]{1,0:T(8,128)S(1)} %convolution_add_fusion.6) | copy-start | bytes 49156
  9.2 5.4 copy-start.34
  18.6 27.6 %copy-start.15 = (f32[128,128,1,1]{1,0,2,3:T(8,128)}, f32[128,128,1,1]{1,0,2,3:T(8,128)S(1)}, u32[]{:S(2)}) copy-start(f32[128,128,1,1]{1,0,2,3:T(8,128)S(1)} %reshape.205) | copy-start | bytes 196612
  20.5 7.9 %copy-start.3 = (f32[32,8,8,128]{3,2,1,0:T(8,128)}, f32[32,8,8,128]{3,2,1,0:T(8,128)S(1)}, u32[]{:S(2)}) copy-start(f32[32,8,8,128]{3,2,1,0:T(8,128)S(1)} %copy.211) | copy-start | bytes 3145732
  25.2 3.2 copy-start.22
  25.4 2.3 copy-start.5
  29.2 4.1 copy-start.17
  33.3 12.3 %copy-start.20 = (f32[128,128,1,1]{1,0,2,3:T(8,128)}, f32[128,128,1,1]{1,0,2,3:T(8,128)S(1)}, u32[]{:S(2)}) copy-start(f32[128,128,1,1]{1,0,2,3:T(8,128)S(1)} %reshape.207) | copy-start | bytes 196612
  120.3 1.6 copy-start
  196.8 2.8 copy-start.19
  259.0 1.6 copy-start.1
  327.0 1.6 copy-start.10
  328.6 2.3 copy-start.14
  418.7 1.3 copy-start.2
  453.8 11.8 %copy-start.23 = (f32[128,128,1,1]{1,0,2,3:T(8,128)S(1)}, f32[128,128,1,1]{1,0,2,3:T(8,128)}, u32[]{:S(2)}) copy-start(f32[128,128,1,1]{1,0,2,3:T(8,128)} %copy-done.22) | copy-start | bytes 196612
  465.6 1.6 copy-start.12
  479.5 11.8 %copy-start.16 = (f32[128,128,1,1]{1,0,2,3:T(8,128)S(1)}, f32[128,128,1,1]{1,0,2,3:T(8,128)}, u32[]{:S(2)}) copy-start(f32[128,128,1,1]{1,0,2,3:T(8,128)} %copy-done.15) | copy-start | bytes 196612
  491.3 3.0 copy-start.11
  491.3 2.2 copy-start.6
  491.3 3.0 copy-start.13
  494.9 2.9 copy-start.4
  496.8 1.0 copy-start.7
  507.1 1.2 copy-start.8
  514.9 3.2 copy-start.33
  514.9 3.2 copy-start.35
  514.9 3.2 copy-start.27
  514.9 3.2 copy-start.29
  514.9 3.4 copy-start.25
  514.9 3.4 copy-start.31
  514.9 32.6 %copy-start.9 = (f32[2,128,8,128]{3,1,2,0:T(8,128)S(1)}, f32[2,128,8,128]{3,1,2,0:T(8,128)}, u32[]{:S(2)}) copy-start(f32[2,128,8,128]{3,1,2,0:T(8,128)} %copy-done.7) | copy-start | bytes 3145732
  518.0 30.5 %copy-start.21 = (f32[128,128,1,1]{1,0,2,3:T(8,128)S(1)}, f32[128,128,1,1]{1,0,2,3:T(8,128)}, u32[]{:S(2)}) copy-start(f32[128,128,1,1]{1,0,2,3:T(8,128)} %copy-done.20) | copy-start | bytes 196612
  557.4 1.2 copy-start.18
  (4 other events, 3.3 us)

commit v2 on v1

v2 whole, which is shorter than its diff:
```python
import functools

import jax
import jax.numpy as jnp
from jax import lax
from jax.experimental import pallas as pl
from jax.experimental.pallas import tpu as pltpu
from jax.sharding import PartitionSpec as P

LEVELS = 64
TILES = 256
MESH = pl.DeviceIdType.MESH
HIGHEST = lax.Precision.HIGHEST
F32 = jnp.float32
BF16 = jnp.bfloat16
NN = ((1,), (0,))
NT = ((1,), (1,))


def dot(a, b, dims=NN, precision=None):
    return lax.dot_general(a, b, (dims, ((), ())), precision=precision, preferred_element_type=F32)


def split(x):
    high = x.astype(BF16)
    return high, (x - high.astype(F32)).astype(BF16)


def dot3(a, b, dims=NN):
    return dot(a[0], b[0], dims) + dot(a[0], b[1], dims) + dot(a[1], b[0], dims)


def roll(x, shift):
    return pltpu.roll(x, shift % 128, 1)


def lane(rows=8):
    return lax.broadcasted_iota(jnp.int32, (rows, 128), 1)


def skew_back(x, shift):
    x = roll(x, -shift)
    row = lax.broadcasted_iota(jnp.int32, x.shape, 0)
    for bit in (1, 2, 4):
        x = jnp.where(row & bit == 0, x, roll(x, -bit))
    return x


def skew(x, shift):
    return pltpu.roll(x, shift % 128, 1, stride=1, stride_axis=0)


def swap_bit(a, b, weight, low):
    return jnp.where(low, a, roll(b, weight)), jnp.where(low, roll(a, -weight), b)


def place():
    g = lax.axis_index("grp")
    d = lax.axis_index("dev")
    return d // 8, d // 4 % 2 * 4 + g // 2, d % 4, g % 2


def target(x, z, y, core):
    return z % 4 * 2 + core, x * 8 + z // 4 * 4 + y


def for_others(act):
    x, z, y, core = place()

    def one(tx, tz, ty, tc):
        g, d = target(tx, tz, ty, tc)
        act(g, d)

    for dz in range(1, 8):
        one(x, (z + dz) % 8, y, core)

    def body(k, carry):
        tx, ty, tc = (x + k % 4) % 4, (y + k // 4 % 4) % 4, (core + k // 16) % 2
        for dz in (0, 4, 1, 5, 2, 6, 3, 7):
            one(tx, (z + dz) % 8, ty, tc)
        return carry

    lax.fori_loop(1, 32, body, 0)


def tile(t):
    return pl.ds(pl.multiple_of(t * 8, 8), 8)


def send_all(send, recv, send_sem, recv_sem):
    me = lax.axis_index("dev") * 8 + lax.axis_index("grp")

    def act(g, d):
        pltpu.make_async_remote_copy(
            src_ref=send.at[tile(d * 8 + g)],
            dst_ref=recv.at[tile(me)],
            send_sem=send_sem,
            recv_sem=recv_sem,
            device_id=(g, d),
            device_id_type=MESH,
        ).start()

    for_others(act)
    recv[tile(me), :] = send[tile(me), :]


def wait_all(ref, sem):
    rest = ref.at[pl.ds(0, 8 * (TILES - 1))]
    pltpu.make_async_copy(rest, rest, sem).wait()


def columns(index, width=128):
    return pl.ds(pl.multiple_of(index * width, width), width)


def pack(field, send, half_diagonal):
    ln = lane()
    first, middle = ln == 0, ln == 64
    low64, low32, low16 = ln < 64, ln & 32 == 0, ln & 16 == 0

    def body(al, carry):
        for bo in range(8):
            v = []
            for a0 in range(2):
                part = []
                for rb in range(2):
                    rows = pl.ds(a0 * 128 + rb * 64 + bo * 8, 8)
                    part.append([skew_back(field[ri, rows, columns(al)], rb * 64 + bo * 8) for ri in range(2)])
                (re0, im0), (re1, im1) = part
                v0 = jnp.where(low64, re0, roll(im0, 64))
                v0 = v0 + jnp.where(first, -im1, jnp.where(middle, roll(re1, 64), 0.0))
                if half_diagonal:
                    v0 = jnp.where(first | middle, 0.5 * v0, v0)
                v1 = jnp.where(low64, re1, roll(im1, 64))
                v1 = jnp.where(first, roll(re0, 64), jnp.where(middle, im0, v1))
                v.append([v0, v1])
            u = [swap_bit(v[0][rb], v[1][rb], 32, low32) for rb in range(2)]
            for h1 in range(2):
                w = swap_bit(u[0][h1], u[1][h1], 16, low16)
                for h0 in range(2):
                    send[pl.ds((h1 * 2 + h0) * 512 + bo * 64 + al, 8, stride=8), :] = w[h0]
        return carry

    lax.fori_loop(0, 8, body, 0)


def unpack(recv, upper, lower):
    ln = lane()
    first, middle = ln == 0, ln == 64
    low64, low32, low16 = ln < 64, ln & 32 == 0, ln & 16 == 0
    inner = low64 & (ln > 0)

    def body(al, carry):
        for bo in range(8):
            t = [recv[pl.ds(h * 512 + bo * 64 + al, 8, stride=8), :] for h in range(4)]
            u = [swap_bit(t[h1 * 2], t[h1 * 2 + 1], 16, low16) for h1 in range(2)]
            v = [swap_bit(u[0][rb], u[1][rb], 32, low32) for rb in range(2)]
            (v00, v10), (v01, v11) = v
            r00, r10, r01, r11 = [roll(q, 64) for q in (v00, v10, v01, v11)]
            zero = jnp.zeros_like(v00)
            ups = [
                [
                    jnp.where(first, 0.5 * (v00 + v10), jnp.where(middle, r01, jnp.where(low64, v00, zero))),
                    jnp.where(first, 0.5 * (r00 - r10), jnp.where(middle, v01, jnp.where(low64, r00, zero))),
                ],
                [
                    jnp.where(first, 0.5 * (r00 + r10), jnp.where(middle, r11, jnp.where(low64, v01, zero))),
                    jnp.where(first, 0.5 * (v10 - v00), jnp.where(middle, -v11, jnp.where(low64, r01, zero))),
                ],
            ]
            downs = [
                [jnp.where(inner, v10, zero), jnp.where(inner, -r10, zero)],
                [jnp.where(inner, v11, zero), jnp.where(inner, -r11, zero)],
            ]
            for rb in range(2):
                base = rb * 64 + bo * 8
                for ri in range(2):
                    upper[ri, pl.ds(base, 8), columns(al)] = skew(ups[rb][ri], base)
                    lower[ri, pl.ds(base, 8), columns(al)] = skew(downs[rb][ri], base)
        return carry

    lax.fori_loop(0, 8, body, 0)


def sign(rows):
    return jnp.where(lane(rows) < 64, -1.0, 1.0).astype(F32)


def mode_one(src, dst, g3, conjugate):
    sgn = sign(64)
    if conjugate:
        sgn = -sgn

    def body(i, carry):
        base = pl.multiple_of(i * 256, 256)
        x = jnp.concatenate([src[pl.ds(base + k * 64, 64), :] for k in range(4)], axis=1)
        high, low = split(x)
        p = dot(g3[...], jnp.concatenate([high, low, high], axis=0))
        for k in range(4):
            q = p[:, k * 128 : k * 128 + 128]
            dst[pl.ds(base + k * 64, 64), :] = q[:64] + sgn * roll(q[64:], 64)
        return carry

    lax.fori_loop(0, 8, body, 0)


def flip(src, dst):
    low32 = lane() & 32 == 0

    def body(c, carry):
        for k in range(4):
            e = [src[pl.ds(k * 512 + c * 2 + bit, 8, stride=64), :] for bit in range(2)]
            o = swap_bit(e[0], e[1], 32, low32)
            for bit in range(2):
                dst[pl.ds(c * 64 + k * 16 + bit, 8, stride=2), :] = o[bit]
        return carry

    lax.fori_loop(0, 32, body, 0)


def gram(x_ref, y_ref, flag):
    sgn = sign(64) * (-flag)

    def body(i, acc):
        for k in range(2):
            base = pl.multiple_of(i * 128 + k * 64, 64)
            x = x_ref[pl.ds(base, 64), :]
            xh, xl = split(jnp.concatenate([x, sgn * roll(x, 64)], axis=0))
            yh, yl = split(y_ref[pl.ds(base, 64), :])
            acc = acc + dot(
                jnp.concatenate([xh, xh, xl, xl], axis=1), jnp.concatenate([yh, yl, yh, yl], axis=1), NT
            )
        return acc

    return lax.fori_loop(0, 16, body, jnp.zeros((128, 64), F32))


def cmul(a, b, dims=NN):
    mul = functools.partial(dot, dims=dims, precision=HIGHEST)
    return mul(a[0], b[0]) - mul(a[1], b[1]), mul(a[0], b[1]) + mul(a[1], b[0])


def conj(a):
    return a[0], -a[1]


def diagonals(u, v, w, m):
    t = cmul(m, conj(v), NT)
    first = jnp.sum(u[0] * m[1] - u[1] * m[0], axis=0, keepdims=True)
    second = jnp.sum(w[0] * t[1] - w[1] * t[0], axis=0, keepdims=True)
    return 2.0 * first, 2.0 * second


def kernel(
    density, costate, phases, displacements, slots, checkpoint, out, grads,
    cin, rin, work, lower, disp, table, send_c, recv_c, send_r, recv_r, send_a, send_b, recv_a, recv_b,
    t1, t2, t3, t4, g3, left_hi, left_lo, right_hi, right_lo, result, tile_ref, near, far,
    load, sem,
):
    loads = []
    for k in range(2):
        loads.append(pltpu.make_async_copy(costate.at[k], cin.at[k], load.at[k]))
    for k in range(2):
        loads.append(pltpu.make_async_copy(density.at[k], rin.at[k], load.at[2 + k]))
    loads.append(pltpu.make_async_copy(displacements, disp, load.at[4]))
    loads.append(pltpu.make_async_copy(phases, table, load.at[5]))
    for copy in loads:
        copy.start()
    barrier = pltpu.get_barrier_semaphore()
    for_others(
        lambda g, d: pl.semaphore_signal(barrier, inc=1, device_id=(g, d), device_id_type=MESH)
    )
    loads[0].wait()
    loads[1].wait()
    pack(cin, send_c, False)
    pl.semaphore_wait(barrier, TILES - 1)
    send_all(send_c, recv_c, sem.at[0], sem.at[1])

    loads[4].wait()
    loads[5].wait()
    start = checkpoint[0]
    first, second = [], []
    for layer in range(2):
        angle = table[slots[start + layer]]
        cosine, sine = jnp.cos(angle), jnp.sin(angle)
        for mode, held in ((0, first), (1, second)):
            re, im = disp[start + layer, mode, 0], disp[start + layer, mode, 1]
            c, s = cosine[mode : mode + 1], sine[mode : mode + 1]
            held.append((re * c - im * s, re * s + im * c))
    va, wa = first
    vb, wb = second
    ua, ub = cmul(wa, va), cmul(wb, vb)
    gh, gl = split(jnp.concatenate([ua[0].T, ua[1].T], axis=0))
    g3[...] = jnp.concatenate([gh, gh, gl], axis=1)
    spread = (
        lax.broadcasted_iota(jnp.int32, (128, 64), 0) // 2 == lax.broadcasted_iota(jnp.int32, (128, 64), 1)
    ).astype(F32)
    parity = (
        lax.broadcasted_iota(jnp.int32, (128, 128), 0) + lax.broadcasted_iota(jnp.int32, (128, 128), 1)
    ) % 2 == 0

    def both(m):
        wide = dot(dot(spread, m, NN, HIGHEST), spread, NT, HIGHEST)
        return jnp.where(parity, wide, 0.0)

    ub, vb, wb = [(both(m[0]), both(m[1])) for m in (ub, vb, wb)]
    left = jnp.concatenate([jnp.concatenate([ub[0], -ub[1]], axis=1), jnp.concatenate([ub[1], ub[0]], axis=1)], axis=0)
    right = jnp.concatenate([jnp.concatenate([ub[0], ub[1]], axis=1), jnp.concatenate([-ub[1], ub[0]], axis=1)], axis=0)
    for k, (m, high, low) in enumerate(((left, left_hi, left_lo), (right, right_hi, right_lo))):
        for turned in range(2):
            h, l = split(m.T if turned else m)
            high[turned], low[turned] = h, l

    loads[2].wait()
    loads[3].wait()

    def rho_body(i, carry):
        wide = columns(i, 256)
        for a0 in range(2):
            rows = pl.ds(a0 * 128, 128)
            x = [rin[ri, rows, wide] for ri in range(2)]
            t = []
            for k in range(2):
                piece = jnp.concatenate([q[:, k * 128 : k * 128 + 128] for q in x], axis=1)
                t.append(dot3(split(piece), (right_hi[1], right_lo[1])))
            t = jnp.concatenate(
                [jnp.concatenate([q[:, :128] for q in t], axis=1), jnp.concatenate([q[:, 128:] for q in t], axis=1)],
                axis=0,
            )
            y = dot3((left_hi[0], left_lo[0]), split(t))
            work[0, rows, wide] = y[:128]
            work[1, rows, wide] = y[128:]
        return carry

    lax.fori_loop(0, 4, rho_body, 0)
    pack(work, send_r, True)
    send_all(send_r, recv_r, sem.at[2], sem.at[3])

    wait_all(recv_c, sem.at[1])
    mode_one(recv_c, t2, g3, False)
    flip(t2, t1)
    mode_one(t1, t2, g3, True)
    flip(t2, t3)
    low32 = lane(64) & 32 == 0

    def blend(i, carry):
        rows = pl.ds(pl.multiple_of(i * 64, 64), 64)
        a, b = swap_bit(t3[rows, :], t2[rows, :], 32, low32)
        send_a[rows, :] = a
        send_b[rows, :] = b
        return carry

    lax.fori_loop(0, 32, blend, 0)
    send_all(send_a, recv_a, sem.at[4], sem.at[5])
    send_all(send_b, recv_b, sem.at[6], sem.at[7])

    flip(recv_c, t2)
    mode_one(t2, t3, g3, True)
    flip(t3, t2)
    wait_all(recv_r, sem.at[3])
    flip(recv_r, t4)
    f = gram(t1, t4, 1.0) + gram(t2, recv_r, -1.0)
    row0, row1 = diagonals(ua, va, wa, (f[:64], f[64:]))

    total = jnp.zeros((256, 256), F32)
    stores = []
    for a0, (recv, number) in enumerate(((recv_a, 5), (recv_b, 7))):
        wait_all(recv, sem.at[number])
        unpack(recv, work, lower)
        rows = pl.ds(a0 * 128, 128)

        def final_body(i, acc, a0=a0, rows=rows):
            wide = columns(i, 256)
            t = []
            for k in range(2):
                chunk = columns(i * 2 + k)
                piece = jnp.concatenate(
                    [work[ri, pl.ds(0, 128), chunk] + lower[ri, :, chunk].T for ri in range(2)], axis=1
                )
                t.append(dot3(split(piece), (right_hi[0], right_lo[0])))
            t = jnp.concatenate(
                [jnp.concatenate([q[:, :128] for q in t], axis=1), jnp.concatenate([q[:, 128:] for q in t], axis=1)],
                axis=0,
            )
            th, tl = split(t)
            y = dot3((left_hi[1], left_lo[1]), (th, tl))
            result[0, rows, wide] = y[:128]
            result[1, rows, wide] = y[128:]
            rh, rl = split(jnp.concatenate([rin[ri, rows, wide] for ri in range(2)], axis=0))
            return acc + dot3((th, tl), (rh, rl), NT) + dot(tl, rl, NT)

        total = lax.fori_loop(0, 4, final_body, total)
        for ri in range(2):
            copy = pltpu.make_async_copy(result.at[ri, rows], out.at[ri, rows], load.at[a0 * 2 + ri])
            copy.start()
            stores.append(copy)
    j = (total[:128, :128] + total[128:, 128:], total[128:, :128] - total[:128, 128:])
    row2, row3 = diagonals(ub, vb, wb, j)
    blank = jnp.zeros((1, 64), F32)
    tile_ref[0] = jnp.concatenate(
        [jnp.concatenate([row0, blank], axis=1), jnp.concatenate([row1, blank], axis=1), row2, row3,
         jnp.zeros((4, 128), F32)], axis=0)

    x, z, y, core = place()
    for half in range(2):
        slots_ref = (near, far)[half]
        for k in range(1, 16):
            if half == 0:
                to = target(x, (z + k // 2) % 8, y, (core + k % 2) % 2)
            else:
                to = target((x + k // 4) % 4, z, (y + k % 4) % 4, core)
            pltpu.make_async_remote_copy(
                src_ref=tile_ref.at[half], dst_ref=slots_ref.at[k - 1], send_sem=sem.at[8 + half],
                recv_sem=sem.at[10 + half], device_id=to, device_id_type=MESH,
            ).start()
        pltpu.make_async_copy(slots_ref, slots_ref, sem.at[10 + half]).wait()
        value = tile_ref[half]
        for k in range(15):
            value = value + slots_ref[k]
        tile_ref[half + 1] = value
    summed = tile_ref[2]
    modes = dot(summed, spread, NN, HIGHEST)
    for layer in range(2):
        grads[layer, 0:1, :] = summed[layer : layer + 1, :64]
        grads[layer, 1:2, :] = modes[2 + layer : 3 + layer, :]
    for half in range(2):
        pltpu.make_async_copy((near, far)[half], (near, far)[half], sem.at[8 + half]).wait()
    wait_all(send_c, sem.at[0])
    wait_all(send_r, sem.at[2])
    wait_all(send_a, sem.at[4])
    wait_all(send_b, sem.at[6])
    for copy in stores:
        copy.wait()


def per_device(density, costate, phases, displacements, table_slot, checkpoint):
    anywhere = pl.BlockSpec(memory_space=pl.ANY)
    smem = pl.BlockSpec(memory_space=pltpu.SMEM)
    tiles = pltpu.VMEM((8 * TILES, 128), F32)
    return pl.pallas_call(
        kernel,
        out_shape=(jax.ShapeDtypeStruct(costate.shape, F32), jax.ShapeDtypeStruct((2, 2, LEVELS), F32)),
        in_specs=[anywhere] * 4 + [smem] * 2,
        out_specs=(anywhere, pl.BlockSpec(memory_space=pltpu.VMEM)),
        scratch_shapes=[
            pltpu.VMEM((2, 256, 1024), F32),
            pltpu.VMEM((2, 256, 1024), F32),
            pltpu.VMEM((2, 256, 1024), F32),
            pltpu.VMEM((2, 128, 1024), F32),
            pltpu.VMEM(displacements.shape, F32),
            pltpu.VMEM(phases.shape, F32),
        ]
        + [tiles] * 8
        + [tiles] * 4
        + [pltpu.VMEM((128, 192), BF16)]
        + [pltpu.VMEM((2, 256, 256), BF16)] * 4
        + [
            pltpu.VMEM((2, 256, 1024), F32),
            pltpu.VMEM((3, 8, 128), F32),
            pltpu.VMEM((15, 8, 128), F32),
            pltpu.VMEM((15, 8, 128), F32),
            pltpu.SemaphoreType.DMA((6,)),
            pltpu.SemaphoreType.DMA((12,)),
        ],
        compiler_params=pltpu.CompilerParams(
            collective_id=0, has_side_effects=True, vmem_limit_bytes=48 * 2**20
        ),
    )(density, costate, phases, displacements, table_slot, checkpoint)


def solution(mesh):
    return jax.shard_map(
        per_device,
        mesh=mesh,
        in_specs=(P(None, "dev", "grp"), P(None, "dev", "grp"), P(), P(), P(), P()),
        out_specs=(P(None, "dev", "grp"), P()),
        check_vma=False,
    )
```

time: 571 us -> 135 us (0.24); the launches traced: 561 us -> 135 us
  local copies, waits for them, and re-layouts: 255 us -> 4.87 us
  Pallas kernels: 215 us -> 128 us
  matrix products: 45.9 us -> 0 us
  other arithmetic: 38 us -> 0 us
    pallas_call x4 -> x1, Pallas kernels: 215 us -> 128 us  [per_device(): pl.pallas_call(kernel, out_shape=(jax.ShapeDtypeStruct(costate.shape, F32...]
    reshape x11 -> x0, local copies, waits for them, and re-layouts: 65.5 us -> none  [the longest x4 26.7 us: there(): f = f.transpose(2, 5, 0, 1, 4, 3, 6).reshape(256, 16, 128)]
    transpose x2 -> x0, local copies, waits for them, and re-layouts: 49.7 us -> none  [there(): f = f.transpose(2, 5, 0, 1, 4, 3, 6).reshape(256, 16, 128)]
    squeeze x4 -> x0, local copies, waits for them, and re-layouts: 48.2 us -> none  [the longest x2 24.1 us: cmul(): a[1]]
    dot_general x48 -> x0, matrix products: 45.9 us -> none  [the longest x12 12.2 us: cmul(): dot(a[1], b[1])]
    another operation x11 -> x0, local copies, waits for them, and re-layouts: 44.7 us -> none  [the longest x10 44.7 us: cmul(): jnp.stack([dot(a[0], b[0]) - dot(a[1], b[1]), dot(a[0], b[1]) + dot(a[1],...]
    transpose x8 -> x0, other arithmetic: 25.8 us -> none  [the longest x1 23.3 us: there(): f = f.transpose(2, 5, 0, 1, 4, 3, 6).reshape(256, 16, 128)]
    slice x5 -> x0, local copies, waits for them, and re-layouts: 16.4 us -> none  [the longest x3 13.7 us: cmul(): a[1]]
where the time goes in v2:
time: 135 us
  Pallas kernels  128 us (95%)
  local copies, waits for them, and re-layouts  4.87 us (4%)
    pallas_call x1, Pallas kernels, per_device(): pl.pallas_call(kernel, out_shape=(jax.ShapeDtypeStruct(costate.shape, F32...  128 us
    unnamed x8, local copies, waits for them, and re-layouts  4.87 us

profile of v2, /device:TPU:1, one launch (start us, length us, event | category | flops | bytes accessed | tf_op | source)
XLA Modules:
  0.0 134.7 jit_solution(6466569552468789509)
XLA Ops:
  1.3 0.0 copy-start
  1.3 1.6 %copy-done = f32[2,256,1024]{2,1,0:T(8,128)S(1)} copy-done((f32[2,256,1024]{2,1,0:T(8,128)S(1)}, f32[2,256,1024]{2,1,0:T(8,128)}, u32[]{:S(2)}) %copy-start) | copy-done | bytes 2097176
  2.9 0.0 copy-start.1
  2.9 0.7 copy-done.1
  3.6 0.0 copy-start.2
  3.6 0.7 copy-done.2
  4.3 128.5 %shard_map.77 = (f32[2,256,1024]{2,1,0:T(8,128)S(1)}, f32[2,2,64]{2,1,0:T(2,128)S(1)}) custom-call(f32[2,256,1024]{2,1,0:T(8,128)S(1)} %copy-done, f32[2,256,1024]{2,1,0:T(8,128)} %costate.1, f32[24,2,64]{2,1,0:T(2,128)S(1)} %copy-done.1, f32[24,2,2,64,64]{4,3,2,1,0:T(8,128)} %displacements.1, s32[24]{0:T(128)S(1)} %copy-done.2, s32[1]{0:T(128)S(6)} %copy.10.checkpoint), custom_call_target="tpu_custom_call" | custom-call | tf_op jit(solution)/shard_map/pallas_call | solution.py:440
  132.8 1.3 copy.11
  134.1 0.6 copy.12
Async XLA Ops:
  1.3 1.6 %copy-start = (f32[2,256,1024]{2,1,0:T(8,128)S(1)}, f32[2,256,1024]{2,1,0:T(8,128)}, u32[]{:S(2)}) copy-start(f32[2,256,1024]{2,1,0:T(8,128)} %density.1) | copy-start | bytes 6291460
  2.9 0.7 copy-start.1
  3.6 0.7 copy-start.2

commit v3 on v2

v3 whole, which is shorter than its diff:
```python
import functools

import jax
import jax.numpy as jnp
from jax import lax
from jax.experimental import pallas as pl
from jax.experimental.pallas import tpu as pltpu
from jax.sharding import PartitionSpec as P

LEVELS = 64
TILES = 256
PITCH = 72
MESH = pl.DeviceIdType.MESH
HIGHEST = lax.Precision.HIGHEST
F32 = jnp.float32
BF16 = jnp.bfloat16
NN = ((1,), (0,))
NT = ((1,), (1,))


def dot(a, b, dims=NN, precision=None):
    return lax.dot_general(a, b, (dims, ((), ())), precision=precision, preferred_element_type=F32)


def split(x):
    high = x.astype(BF16)
    return high, (x - high.astype(F32)).astype(BF16)


def dot3(a, b, dims=NN):
    return dot(a[0], b[0], dims) + dot(a[0], b[1], dims) + dot(a[1], b[0], dims)


def roll(x, shift):
    return pltpu.roll(x, shift % 128, 1)


def lane(rows=8):
    return lax.broadcasted_iota(jnp.int32, (rows, 128), 1)


def swap_bit(a, b, weight, low):
    return jnp.where(low, a, roll(b, weight)), jnp.where(low, roll(a, -weight), b)


def place():
    g = lax.axis_index("grp")
    d = lax.axis_index("dev")
    return d >> 3, ((d >> 2) & 1) * 4 + (g >> 1), d & 3, g & 1


def target(x, z, y, core):
    return (z & 3) * 2 + core, x * 8 + (z >> 2) * 4 + y


def apart(a, b):
    e = (a - b) & 7
    return jnp.minimum(e, 8 - e)


def tile(t):
    return pl.ds(pl.multiple_of(t * 8, 8), 8)


def slot(d, g):
    return pl.ds(pl.multiple_of(d * PITCH + g * 8, 8), 8)


def for_others(act):
    x, z, y, core = place()

    def one(tx, dz, ty, tc):
        g, d = target(tx, (z + dz) & 7, ty, tc)
        act(g, d, dz, (tx + ty + tc) & 1)

    for dz in range(1, 8):
        one(x, dz, y, core)

    def body(k, carry):
        tx, ty, tc = (x + k) & 3, (y + (k >> 2)) & 3, (core + (k >> 4)) & 1
        for dz in (0, 4, 1, 5, 2, 6, 3, 7):
            one(tx, dz, ty, tc)
        return carry

    lax.fori_loop(1, 32, body, 0)


def send_all(send, recv, send_sem, recv_sem):
    me_g, me_d = lax.axis_index("grp"), lax.axis_index("dev")

    def act(g, d, dz, parity):
        pltpu.make_async_remote_copy(
            src_ref=send.at[tile(d * 8 + g)],
            dst_ref=recv.at[tile(me_d * 8 + me_g)],
            send_sem=send_sem,
            recv_sem=recv_sem,
            device_id=(g, d),
            device_id_type=MESH,
        ).start()

    for_others(act)
    recv[tile(me_d * 8 + me_g), :] = send[tile(me_d * 8 + me_g), :]


def send_near(send, recv, send_sem, recv_sem):
    x, z, y, core = place()
    me_g, me_d = lax.axis_index("grp"), lax.axis_index("dev")
    quad = me_d >> 2
    alone = quad == me_g
    after = (quad > me_g).astype(jnp.int32)
    other = core * 4 + x
    nearer = []
    for dz in range(8):
        own, far = min(dz, 8 - dz), apart(other, z + dz)
        nearer.append(jnp.where(far == own, 2, jnp.where(own < far, 1, 0)))

    def copy(order, g, d):
        return pltpu.make_async_remote_copy(
            src_ref=send[order].at[tile(d * 8 + g)],
            dst_ref=recv[order].at[slot(me_d, me_g)],
            send_sem=send_sem.at[order],
            recv_sem=recv_sem.at[order],
            device_id=(g, d),
            device_id_type=MESH,
        )

    def act(g, d, dz, parity):
        chosen = jnp.where(nearer[dz] == 2, parity ^ after, nearer[dz]) == 1

        @pl.when(alone | chosen)
        def _():
            copy(0, g, d).start()

        @pl.when(jnp.logical_not(alone) & chosen)
        def _():
            copy(1, g, d).start()

    for_others(act)
    for order in range(2):
        recv[order][slot(me_d, me_g), :] = send[order][tile(me_d * 8 + me_g), :]


def wait_tiles(ref, sem, count):
    rest = ref.at[pl.ds(0, 8 * count)]
    pltpu.make_async_copy(rest, rest, sem).wait()


def wait_near(recv, recv_sem):
    alone = lax.axis_index("dev") >> 2 == lax.axis_index("grp")
    wait_tiles(recv[0], recv_sem.at[0], 143)
    for flag, count in ((alone, 112), (jnp.logical_not(alone), 111)):

        @pl.when(flag)
        def _(count=count):
            wait_tiles(recv[1], recv_sem.at[1], count)


def wait_near_sent(send, send_sem):
    alone = lax.axis_index("dev") >> 2 == lax.axis_index("grp")

    @pl.when(alone)
    def _():
        wait_tiles(send[0], send_sem.at[0], 255)

    @pl.when(jnp.logical_not(alone))
    def _():
        wait_tiles(send[0], send_sem.at[0], 127)
        wait_tiles(send[1], send_sem.at[1], 127)


def columns(index, width=128):
    return pl.ds(pl.multiple_of(index * width, width), width)


def masks(bo):
    ln = lane()
    window = (ln >= 8 * bo) & (ln < 8 * bo + 64)
    diagonal = ((ln & 63) >= 8 * bo) & ((ln & 63) < 8 * bo + 8)
    return ln < 64, ln & 32 == 0, window, diagonal


def quarter(rows=8):
    return jnp.where(lane(rows) < 64, -1.0, 1.0).astype(F32)


def pack(field, send, half_diagonal):
    sgn = quarter()

    def body(al, carry):
        for bo in range(8):
            low64, low32, window, diagonal = masks(bo)
            v = [[], []]
            for a0 in range(2):
                folded = []
                for rb in range(2):
                    rows = pl.ds(a0 * 128 + rb * 64 + bo * 8, 8)
                    re, im = [field[ri, rows, columns(al)] for ri in range(2)]
                    a = jnp.where(low64, re, im)
                    b = roll(jnp.where(low64, im, re), 64)
                    keep = window if rb == 0 else jnp.logical_not(window)
                    folded.append(jnp.where(keep, a, b))
                    if rb == 0:
                        rest = jnp.where(window, b, a)
                k = folded[0] + sgn * roll(folded[1], 64)
                if half_diagonal:
                    k = 0.5 * k
                v[0].append(jnp.where(diagonal, k, folded[0]))
                v[1].append(jnp.where(diagonal, rest, folded[1]))
            for rb in range(2):
                w = swap_bit(v[rb][0], v[rb][1], 32, low32)
                for h in range(2):
                    send[pl.ds(h * 1024 + rb * 512 + bo * 64 + al, 8, stride=8), :] = w[h]
        return carry

    lax.fori_loop(0, 8, body, 0)


def turn_over(field, dst):
    def body(al, carry):
        for a0 in range(2):
            rows = pl.ds(a0 * 128, 128)
            dst[0, rows, columns(al)] = field[0, rows, columns(al)].T
            dst[1, rows, columns(al)] = -(field[1, rows, columns(al)].T)
        return carry

    lax.fori_loop(0, 8, body, 0)


def unpack(recv, upper, lower):
    sgn = quarter()

    def body(al, carry):
        for bo in range(8):
            low64, low32, window, diagonal = masks(bo)
            outside = diagonal & jnp.logical_not(low64)
            v = []
            for rb in range(2):
                t = [recv[pl.ds(h * 1024 + rb * 512 + bo * 64 + al, 8, stride=8), :] for h in range(2)]
                v.append(swap_bit(t[0], t[1], 32, low32))
            for order, dst in ((0, upper), (1, lower)):
                v0, v1 = v[0][order], v[1][order]
                if order == 1:
                    v0, v1 = -sgn * v0, -sgn * v1
                r0, r1 = roll(v0, 64), roll(v1, 64)
                way = -0.5 if order == 0 else 0.5
                u0, s0 = jnp.where(diagonal, 0.5 * v0, v0), jnp.where(diagonal, 0.5 * r0, r0)
                u1, s1 = jnp.where(diagonal, way * sgn * r0, v1), jnp.where(diagonal, -way * sgn * v0, r1)
                rows = pl.ds(bo * 8, 8)
                dst[0, rows, columns(al)] = jnp.where(window, jnp.where(low64, u0, s0), jnp.where(outside, r1, 0.0))
                dst[1, rows, columns(al)] = jnp.where(window, jnp.where(low64, s0, u0), jnp.where(outside, v1, 0.0))
                rows = pl.ds(64 + bo * 8, 8)
                dst[0, rows, columns(al)] = jnp.where(window, 0.0, jnp.where(low64, u1, s1))
                dst[1, rows, columns(al)] = jnp.where(window, 0.0, jnp.where(low64, s1, u1))
        return carry

    lax.fori_loop(0, 8, body, 0)


def mode_one(src, dst, g3, conjugate):
    sgn = quarter(64)
    if conjugate:
        sgn = -sgn

    def body(i, carry):
        base = pl.multiple_of(i * (8 * PITCH), 8)
        for j in range(2):
            rows = [pl.ds(base + (4 * j + k) * PITCH, 64) for k in range(4)]
            x = jnp.concatenate([src[r, :] for r in rows], axis=1)
            high, low = split(x)
            p = dot(g3[...], jnp.concatenate([high, low, high], axis=0))
            for k in range(4):
                q = p[:, k * 128 : k * 128 + 128]
                dst[rows[k], :] = q[:64] + sgn * roll(q[64:], 64)
        return carry

    lax.fori_loop(0, 4, body, 0)


def sent_direct(quad, k, alone):
    x, z, y, core = place()
    g = 2 * k + (lax.broadcasted_iota(jnp.int32, (8, 128), 0) >> 2)
    own = apart((quad & 1) * 4 + (g >> 1), z)
    far = apart((g & 1) * 4 + (quad >> 1), z)
    parity = (x + y + core) & 1
    tie = jnp.where(quad > g, 1, 0) != parity
    chosen = (own < far) | ((own == far) & tie)
    return (quad == g) | chosen if alone else (quad != g) & chosen


def flip(src, dst, direct=None, alone=True):
    low32 = lane() & 32 == 0

    def body(quad, carry):
        for k in range(4):
            if direct is not None:
                keep = sent_direct(quad, k, alone)
            for j in range(4):
                c = quad * 4 + j
                e = [src[pl.ds(k * (8 * PITCH) + c * 2 + bit, 8, stride=PITCH), :] for bit in range(2)]
                o = swap_bit(e[0], e[1], 32, low32)
                for bit in range(2):
                    rows = pl.ds(c * PITCH + k * 16 + bit, 8, stride=2)
                    value = o[bit]
                    if direct is not None:
                        value = jnp.where(keep, direct[rows, :], value)
                    dst[rows, :] = value
        return carry

    lax.fori_loop(0, 8, body, 0)


def blend(y1, y2, send_a, send_b):
    low32 = lane(64) & 32 == 0

    def body(i, carry):
        for k in range(4):
            c = i * 4 + k
            held = pl.ds(pl.multiple_of(c * PITCH, 8), 64)
            rows = pl.ds(pl.multiple_of(c * 64, 64), 64)
            send_a[rows, :], send_b[rows, :] = swap_bit(y1[held, :], y2[held, :], 32, low32)
        return carry

    lax.fori_loop(0, 8, body, 0)


def gram(x_ref, y_ref, flag):
    sgn = quarter(64) * (-flag)

    def body(i, acc):
        xs, ys = [], []
        for k in range(4):
            rows = pl.ds(pl.multiple_of(i * (4 * PITCH), 8) + k * PITCH, 64)
            x = x_ref[rows, :]
            xh, xl = split(jnp.concatenate([x, sgn * roll(x, 64)], axis=0))
            yh, yl = split(y_ref[rows, :])
            xs += [xh, xh, xl, xl]
            ys += [yh, yl, yh, yl]
        return acc + dot(jnp.concatenate(xs, axis=1), jnp.concatenate(ys, axis=1), NT)

    return lax.fori_loop(0, 8, body, jnp.zeros((128, 64), F32))


def cmul(a, b, dims=NN):
    mul = functools.partial(dot, dims=dims, precision=HIGHEST)
    return mul(a[0], b[0]) - mul(a[1], b[1]), mul(a[0], b[1]) + mul(a[1], b[0])


def conj(a):
    return a[0], -a[1]


def diagonals(u, v, w, m):
    t = cmul(m, conj(v), NT)
    first = jnp.sum(u[0] * m[1] - u[1] * m[0], axis=0, keepdims=True)
    second = jnp.sum(w[0] * t[1] - w[1] * t[0], axis=0, keepdims=True)
    return 2.0 * first, 2.0 * second


def across(x, right_hi, right_lo):
    t = []
    for k in range(2):
        piece = jnp.concatenate([q[:, k * 128 : k * 128 + 128] for q in x], axis=1)
        t.append(dot3(split(piece), (right_hi, right_lo)))
    return [jnp.concatenate([q[:, half * 128 : half * 128 + 128] for q in t], axis=1) for half in range(2)]


def rho_stage(rin, work, right_hi, right_lo, left_hi, left_lo):
    def body(i, carry):
        wide = columns(i, 256)
        t = across([rin[ri, :, wide] for ri in range(2)], right_hi[1], right_lo[1])
        for a0 in range(2):
            rows = pl.ds(a0 * 128, 128)
            y = dot3(
                (left_hi[0], left_lo[0]),
                split(jnp.concatenate([q[a0 * 128 : a0 * 128 + 128] for q in t], axis=0)),
            )
            work[0, rows, wide] = y[:128]
            work[1, rows, wide] = y[128:]
        return carry

    lax.fori_loop(0, 4, body, 0)


def final_stage(work, lower, rin, right_hi, right_lo, left_hi, left_lo, result, rows, total):
    def body(i, acc):
        wide = columns(i, 256)
        x = [
            jnp.concatenate(
                [work[ri, pl.ds(0, 128), columns(i * 2 + k)] + lower[ri, :, columns(i * 2 + k)].T for k in range(2)],
                axis=1,
            )
            for ri in range(2)
        ]
        th, tl = split(jnp.concatenate(across(x, right_hi[0], right_lo[0]), axis=0))
        y = dot3((left_hi[1], left_lo[1]), (th, tl))
        result[0, rows, wide] = y[:128]
        result[1, rows, wide] = y[128:]
        rh, rl = split(jnp.concatenate([rin[ri, rows, wide] for ri in range(2)], axis=0))
        return acc + dot3((th, tl), (rh, rl), NT) + dot(tl, rl, NT)

    return lax.fori_loop(0, 4, body, total)


def kernel(
    density, costate, phases, displacements, slots_hbm, checkpoint_hbm, out, grads,
    result, cin, rin, work, turned, lower, disp, table, slots, checkpoint,
    c_send0, c_send1, r_send0, r_send1, c_recv0, c_recv1, r_recv0, r_recv1, send_a, send_b, recv_a, recv_b,
    t1, t2, t3, t4, g3, left_hi, left_lo, right_hi, right_lo, tile_ref, near, far,
    ready, load, sem,
):
    c_send, r_send = (c_send0, c_send1), (r_send0, r_send1)
    c_recv, r_recv = (c_recv0, c_recv1), (r_recv0, r_recv1)
    x, z, y, core = place()
    loads = [
        pltpu.make_async_copy(costate.at[0], cin.at[0], load.at[0]),
        pltpu.make_async_copy(costate.at[1], cin.at[1], load.at[1]),
        pltpu.make_async_copy(density.at[0], rin.at[0], load.at[2]),
        pltpu.make_async_copy(density.at[1], rin.at[1], load.at[3]),
        pltpu.make_async_copy(displacements, disp, load.at[4]),
        pltpu.make_async_copy(phases, table, load.at[5]),
        pltpu.make_async_copy(slots_hbm, slots, load.at[6]),
        pltpu.make_async_copy(checkpoint_hbm, checkpoint, load.at[7]),
    ]
    for copy in loads:
        copy.start()
    ring = [target(x, (z + k // 2) & 7, y, (core + k % 2) & 1) for k in range(1, 16)]
    plane = [target((x + k // 4) & 3, z, (y + k % 4) & 3, core) for k in range(1, 16)]
    barrier = pltpu.get_barrier_semaphore()
    for to in ring + plane:
        pl.semaphore_signal(barrier, inc=1, device_id=to, device_id_type=MESH)
    loads[0].wait()
    loads[1].wait()
    pack(cin, c_send0, False)
    pl.semaphore_wait(barrier, 30)
    for to in plane:
        pl.semaphore_signal(ready, inc=1, device_id=to, device_id_type=MESH)
    turn_over(cin, turned)
    pack(turned, c_send1, False)
    pl.semaphore_wait(ready, 15)
    c_sems = (sem.at[pl.ds(0, 2)], sem.at[pl.ds(2, 2)])
    r_sems = (sem.at[pl.ds(4, 2)], sem.at[pl.ds(6, 2)])
    send_near(c_send, c_recv, *c_sems)

    for copy in loads[4:]:
        copy.wait()
    start = checkpoint[0]
    first, second = [], []
    for layer in range(2):
        angle = table[slots[start + layer]]
        cosine, sine = jnp.cos(angle), jnp.sin(angle)
        for mode, held in ((0, first), (1, second)):
            re, im = disp[start + layer, mode, 0], disp[start + layer, mode, 1]
            c, s = cosine[mode : mode + 1], sine[mode : mode + 1]
            held.append((re * c - im * s, re * s + im * c))
    va, wa = first
    vb, wb = second
    ua, ub = cmul(wa, va), cmul(wb, vb)
    gh, gl = split(jnp.concatenate([ua[0].T, ua[1].T], axis=0))
    g3[...] = jnp.concatenate([gh, gh, gl], axis=1)
    spread = (
        lax.broadcasted_iota(jnp.int32, (128, 64), 0) // 2 == lax.broadcasted_iota(jnp.int32, (128, 64), 1)
    ).astype(F32)
    parity = (
        lax.broadcasted_iota(jnp.int32, (128, 128), 0) + lax.broadcasted_iota(jnp.int32, (128, 128), 1)
    ) % 2 == 0

    def both(m):
        wide = dot(dot(spread, m, NN, HIGHEST), spread, NT, HIGHEST)
        return jnp.where(parity, wide, 0.0)

    ub, vb, wb = [(both(m[0]), both(m[1])) for m in (ub, vb, wb)]
    left = jnp.concatenate([jnp.concatenate([ub[0], -ub[1]], axis=1), jnp.concatenate([ub[1], ub[0]], axis=1)], axis=0)
    right = jnp.concatenate([jnp.concatenate([ub[0], ub[1]], axis=1), jnp.concatenate([-ub[1], ub[0]], axis=1)], axis=0)
    for m, high, low in ((left, left_hi, left_lo), (right, right_hi, right_lo)):
        for other in range(2):
            high[other], low[other] = split(m.T if other else m)

    loads[2].wait()
    loads[3].wait()
    rho_stage(rin, work, right_hi, right_lo, left_hi, left_lo)
    pack(work, r_send0, True)
    turn_over(work, turned)
    pack(turned, r_send1, True)
    send_near(r_send, r_recv, *r_sems)

    wait_near(c_recv, c_sems[1])
    flip(c_recv1, t1, c_recv0)
    mode_one(t1, t2, g3, False)
    flip(t2, t1)
    mode_one(t1, t2, g3, True)
    flip(t2, t3)
    blend(t3, t2, send_a, send_b)
    send_all(send_a, recv_a, sem.at[8], sem.at[9])
    send_all(send_b, recv_b, sem.at[10], sem.at[11])

    flip(c_recv0, t2, c_recv1, False)
    mode_one(t2, t3, g3, True)
    flip(t3, t2)
    wait_near(r_recv, r_sems[1])
    flip(r_recv1, t3, r_recv0)
    flip(t3, t4)
    f = gram(t1, t4, 1.0) + gram(t2, t3, -1.0)
    row0, row1 = diagonals(ua, va, wa, (f[:64], f[64:]))

    total = jnp.zeros((256, 256), F32)
    stores = []
    for a0, (recv, number) in enumerate(((recv_a, 9), (recv_b, 11))):
        wait_tiles(recv, sem.at[number], TILES - 1)
        unpack(recv, work, lower)
        total = final_stage(
            work, lower, rin, right_hi, right_lo, left_hi, left_lo, result, pl.ds(a0 * 128, 128), total
        )
        for ri in range(2):
            rows = pl.ds(a0 * 128, 128)
            copy = pltpu.make_async_copy(result.at[ri, rows], out.at[ri, rows], load.at[a0 * 2 + ri])
            copy.start()
            stores.append(copy)
    j = (total[:128, :128] + total[128:, 128:], total[128:, :128] - total[:128, 128:])
    row2, row3 = diagonals(ub, vb, wb, j)
    blank = jnp.zeros((1, 64), F32)
    tile_ref[0] = jnp.concatenate(
        [jnp.concatenate([row0, blank], axis=1), jnp.concatenate([row1, blank], axis=1), row2, row3,
         jnp.zeros((4, 128), F32)], axis=0)

    for half, (group, held) in enumerate(((ring, near), (plane, far))):
        for k, to in enumerate(group):
            pltpu.make_async_remote_copy(
                src_ref=tile_ref.at[half], dst_ref=held.at[k], send_sem=sem.at[12 + half],
                recv_sem=sem.at[14 + half], device_id=to, device_id_type=MESH,
            ).start()
        pltpu.make_async_copy(held, held, sem.at[14 + half]).wait()
        value = tile_ref[half]
        for k in range(15):
            value = value + held[k]
        tile_ref[half + 1] = value
    summed = tile_ref[2]
    modes = dot(summed, spread, NN, HIGHEST)
    for layer in range(2):
        grads[layer, 0:1, :] = summed[layer : layer + 1, :64]
        grads[layer, 1:2, :] = modes[2 + layer : 3 + layer, :]
    for half, held in enumerate((near, far)):
        pltpu.make_async_copy(held, held, sem.at[12 + half]).wait()
    wait_near_sent(c_send, c_sems[0])
    wait_near_sent(r_send, r_sems[0])
    wait_tiles(send_a, sem.at[8], TILES - 1)
    wait_tiles(send_b, sem.at[10], TILES - 1)
    for copy in stores:
        copy.wait()


def per_device(density, costate, phases, displacements, table_slot, checkpoint):
    anywhere = pl.BlockSpec(memory_space=pl.ANY)
    vmem = pl.BlockSpec(memory_space=pltpu.VMEM)
    field = pltpu.VMEM((2, 256, 1024), F32)
    tiles = pltpu.VMEM((8 * TILES, 128), F32)
    spaced = pltpu.VMEM((32 * PITCH, 128), F32)
    matrix = pltpu.VMEM((2, 256, 256), BF16)
    return pl.pallas_call(
        kernel,
        out_shape=(jax.ShapeDtypeStruct(costate.shape, F32), jax.ShapeDtypeStruct((2, 2, LEVELS), F32)),
        in_specs=[anywhere] * 6,
        out_specs=(anywhere, vmem),
        scratch_shapes=[field] * 5
        + [
            pltpu.VMEM((2, 128, 1024), F32),
            pltpu.VMEM(displacements.shape, F32),
            pltpu.VMEM(phases.shape, F32),
            pltpu.SMEM(table_slot.shape, jnp.int32),
            pltpu.SMEM(checkpoint.shape, jnp.int32),
        ]
        + [tiles] * 4 + [spaced] * 4 + [tiles] * 4 + [spaced] * 4
        + [pltpu.VMEM((128, 192), BF16)]
        + [matrix] * 4
        + [
            pltpu.VMEM((3, 8, 128), F32),
            pltpu.VMEM((15, 8, 128), F32),
            pltpu.VMEM((15, 8, 128), F32),
            pltpu.SemaphoreType.REGULAR,
            pltpu.SemaphoreType.DMA((8,)),
            pltpu.SemaphoreType.DMA((16,)),
        ],
        compiler_params=pltpu.CompilerParams(
            collective_id=0, has_side_effects=True, vmem_limit_bytes=52 * 2**20
        ),
    )(density, costate, phases, displacements, table_slot, checkpoint)


def solution(mesh):
    return jax.shard_map(
        per_device,
        mesh=mesh,
        in_specs=(P(None, "dev", "grp"), P(None, "dev", "grp"), P(), P(), P(), P()),
        out_specs=(P(None, "dev", "grp"), P()),
        check_vma=False,
    )
```

time: 135 us -> 118 us (0.87)
  Pallas kernels: 128 us -> 112 us
    pallas_call x1, Pallas kernels: 128 us -> 112 us  [per_device(): pl.pallas_call(kernel, out_shape=(jax.ShapeDtypeStruct(costate.shape, F32...]
    unnamed x8 -> x6, local copies, waits for them, and re-layouts: 4.87 us -> 5.12 us
where the time goes in v3:
time: 118 us
  Pallas kernels  112 us (95%)
  local copies, waits for them, and re-layouts  5.12 us (4%)
  between operations  1.3 us (1%)
    pallas_call x1, Pallas kernels, per_device(): pl.pallas_call(kernel, out_shape=(jax.ShapeDtypeStruct(costate.shape, F32...  112 us
    unnamed x6, local copies, waits for them, and re-layouts  5.12 us

profile of v3, /device:TPU:1, one launch (start us, length us, event | category | flops | bytes accessed | tf_op | source)
XLA Modules:
  0.0 118.2 jit_solution(11546258651505836352)
XLA Ops:
  1.3 0.0 copy-start
  1.3 0.7 copy-done
  2.0 0.0 copy-start.1
  2.0 0.7 copy-done.1
  2.7 111.8 %shard_map.77 = (f32[2,256,1024]{2,1,0:T(8,128)}, f32[2,2,64]{2,1,0:T(2,128)S(1)}) custom-call(f32[2,256,1024]{2,1,0:T(8,128)} %density.1, f32[2,256,1024]{2,1,0:T(8,128)} %costate.1, f32[24,2,64]{2,1,0:T(2,128)S(1)} %copy-done, f32[24,2,2,64,64]{4,3,2,1,0:T(8,128)} %displacements.1, s32[24]{0:T(128)S(1)} %copy-done.1, s32[1]{0:T(128)S(6)} %copy.10.checkpoint_hbm), custom_call_target="tpu_custom_call" | custom-call | tf_op jit(solution)/shard_map/pallas_call | solution.py:558
  114.5 3.2 %copy.11 = f32[2,256,1024]{2,1,0:T(8,128)} copy(f32[2,256,1024]{2,1,0:T(8,128)} %get-tuple-element.4) | data formatting | bytes 4194304
  117.7 0.6 copy.12
Async XLA Ops:
  1.3 0.7 copy-start
  2.0 0.7 copy-start.1

commit v4 on v3

--- a/solution.py
+++ b/solution.py
@@ -66,31 +66,48 @@
     return pl.ds(pl.multiple_of(d * PITCH + g * 8, 8), 8)
 
 
-def for_others(act):
+def visit(act, k, steps):
     x, z, y, core = place()
-
-    def one(tx, dz, ty, tc):
+    tx, ty, tc = (x + k) & 3, (y + (k >> 2)) & 3, (core + (k >> 4)) & 1
+    for dz in steps:
         g, d = target(tx, (z + dz) & 7, ty, tc)
         act(g, d, dz, (tx + ty + tc) & 1)
 
-    for dz in range(1, 8):
-        one(x, dz, y, core)
-
+
+ALL = (0, 4, 1, 5, 2, 6, 3, 7)
+AWAY = (4, 1, 5, 2, 6, 3, 7)
+
+
+def visit_range(act, low, high, steps=ALL):
     def body(k, carry):
-        tx, ty, tc = (x + k) & 3, (y + (k >> 2)) & 3, (core + (k >> 4)) & 1
-        for dz in (0, 4, 1, 5, 2, 6, 3, 7):
-            one(tx, dz, ty, tc)
-        return carry
-
-    lax.fori_loop(1, 32, body, 0)
-
-
-def send_all(send, recv, send_sem, recv_sem):
+        visit(act, k, steps)
+        return carry
+
+    lax.fori_loop(low, high, body, 0)
+
+
+def for_first(act):
+    visit(act, 0, AWAY)
+    visit(act, 16, ALL)
+    visit_range(act, 1, 16, (0,))
+
+
+def for_rest(act):
+    visit_range(act, 1, 16, AWAY)
+    visit_range(act, 17, 32)
+
+
+def for_others(act):
+    visit(act, 0, AWAY)
+    visit_range(act, 1, 32)
+
+
+def send_some(send, recv, send_sem, recv_sem, low, high):
     me_g, me_d = lax.axis_index("grp"), lax.axis_index("dev")
 
     def act(g, d, dz, parity):
         pltpu.make_async_remote_copy(
-            src_ref=send.at[tile(d * 8 + g)],
+            src_ref=send.at[slot(d, g)],
             dst_ref=recv.at[tile(me_d * 8 + me_g)],
             send_sem=send_sem,
             recv_sem=recv_sem,
@@ -98,11 +115,13 @@
             device_id_type=MESH,
         ).start()
 
-    for_others(act)
-    recv[tile(me_d * 8 + me_g), :] = send[tile(me_d * 8 + me_g), :]
-
-
-def send_near(send, recv, send_sem, recv_sem):
+    if low == 0:
+        visit(act, 0, AWAY)
+        recv[tile(me_d * 8 + me_g), :] = send[slot(me_d, me_g), :]
+    visit_range(act, max(low, 1), high)
+
+
+def send_near(order, send, recv, send_sem, recv_sem, visits):
     x, z, y, core = place()
     me_g, me_d = lax.axis_index("grp"), lax.axis_index("dev")
     quad = me_d >> 2
@@ -114,30 +133,23 @@
         own, far = min(dz, 8 - dz), apart(other, z + dz)
         nearer.append(jnp.where(far == own, 2, jnp.where(own < far, 1, 0)))
 
-    def copy(order, g, d):
-        return pltpu.make_async_remote_copy(
-            src_ref=send[order].at[tile(d * 8 + g)],
-            dst_ref=recv[order].at[slot(me_d, me_g)],
-            send_sem=send_sem.at[order],
-            recv_sem=recv_sem.at[order],
-            device_id=(g, d),
-            device_id_type=MESH,
-        )
-
     def act(g, d, dz, parity):
         chosen = jnp.where(nearer[dz] == 2, parity ^ after, nearer[dz]) == 1
 
-        @pl.when(alone | chosen)
+        @pl.when(alone | chosen if order == 0 else jnp.logical_not(alone) & chosen)
         def _():
-            copy(0, g, d).start()
-
-        @pl.when(jnp.logical_not(alone) & chosen)
-        def _():
-            copy(1, g, d).start()
-
-    for_others(act)
-    for order in range(2):
-        recv[order][slot(me_d, me_g), :] = send[order][tile(me_d * 8 + me_g), :]
+            pltpu.make_async_remote_copy(
+                src_ref=send[order].at[tile(d * 8 + g)],
+                dst_ref=recv[order].at[slot(me_d, me_g)],
+                send_sem=send_sem.at[order],
+                recv_sem=recv_sem.at[order],
+                device_id=(g, d),
+                device_id_type=MESH,
+            ).start()
+
+    for each in visits:
+        each(act)
+    recv[order][slot(me_d, me_g), :] = send[order][tile(me_d * 8 + me_g), :]
 
 
 def wait_tiles(ref, sem, count):
@@ -226,8 +238,9 @@
     lax.fori_loop(0, 8, body, 0)
 
 
-def unpack(recv, upper, lower):
+def unpack(recv, dst, turned):
     sgn = quarter()
+    way = 0.5 if turned else -0.5
 
     def body(al, carry):
         for bo in range(8):
@@ -237,18 +250,17 @@
             for rb in range(2):
                 t = [recv[pl.ds(h * 1024 + rb * 512 + bo * 64 + al, 8, stride=8), :] for h in range(2)]
                 v.append(swap_bit(t[0], t[1], 32, low32))
-            for order, dst in ((0, upper), (1, lower)):
-                v0, v1 = v[0][order], v[1][order]
-                if order == 1:
+            for a0 in range(2):
+                v0, v1 = v[0][a0], v[1][a0]
+                if turned:
                     v0, v1 = -sgn * v0, -sgn * v1
                 r0, r1 = roll(v0, 64), roll(v1, 64)
-                way = -0.5 if order == 0 else 0.5
                 u0, s0 = jnp.where(diagonal, 0.5 * v0, v0), jnp.where(diagonal, 0.5 * r0, r0)
                 u1, s1 = jnp.where(diagonal, way * sgn * r0, v1), jnp.where(diagonal, -way * sgn * v0, r1)
-                rows = pl.ds(bo * 8, 8)
+                rows = pl.ds(a0 * 128 + bo * 8, 8)
                 dst[0, rows, columns(al)] = jnp.where(window, jnp.where(low64, u0, s0), jnp.where(outside, r1, 0.0))
                 dst[1, rows, columns(al)] = jnp.where(window, jnp.where(low64, s0, u0), jnp.where(outside, v1, 0.0))
-                rows = pl.ds(64 + bo * 8, 8)
+                rows = pl.ds(a0 * 128 + 64 + bo * 8, 8)
                 dst[0, rows, columns(al)] = jnp.where(window, 0.0, jnp.where(low64, u1, s1))
                 dst[1, rows, columns(al)] = jnp.where(window, 0.0, jnp.where(low64, s1, u1))
         return carry
@@ -309,20 +321,6 @@
     lax.fori_loop(0, 8, body, 0)
 
 
-def blend(y1, y2, send_a, send_b):
-    low32 = lane(64) & 32 == 0
-
-    def body(i, carry):
-        for k in range(4):
-            c = i * 4 + k
-            held = pl.ds(pl.multiple_of(c * PITCH, 8), 64)
-            rows = pl.ds(pl.multiple_of(c * 64, 64), 64)
-            send_a[rows, :], send_b[rows, :] = swap_bit(y1[held, :], y2[held, :], 32, low32)
-        return carry
-
-    lax.fori_loop(0, 8, body, 0)
-
-
 def gram(x_ref, y_ref, flag):
     sgn = quarter(64) * (-flag)
 
@@ -370,10 +368,7 @@
         t = across([rin[ri, :, wide] for ri in range(2)], right_hi[1], right_lo[1])
         for a0 in range(2):
             rows = pl.ds(a0 * 128, 128)
-            y = dot3(
-                (left_hi[0], left_lo[0]),
-                split(jnp.concatenate([q[a0 * 128 : a0 * 128 + 128] for q in t], axis=0)),
-            )
+            y = dot3((left_hi[0], left_lo[0]), split(jnp.concatenate(halves(t, a0), axis=0)))
             work[0, rows, wide] = y[:128]
             work[1, rows, wide] = y[128:]
         return carry
@@ -381,31 +376,66 @@
     lax.fori_loop(0, 4, body, 0)
 
 
-def final_stage(work, lower, rin, right_hi, right_lo, left_hi, left_lo, result, rows, total):
+def halves(x, a0):
+    return [q[a0 * 128 : a0 * 128 + 128] for q in x]
+
+
+def lower_stage(lower, rin, right_hi, right_lo, left_hi, left_lo, result):
     def body(i, acc):
+        first, second = acc
         wide = columns(i, 256)
+        e = [lower[ri, :, wide] for ri in range(2)]
         x = [
             jnp.concatenate(
-                [work[ri, pl.ds(0, 128), columns(i * 2 + k)] + lower[ri, :, columns(i * 2 + k)].T for k in range(2)],
-                axis=1,
+                [
+                    jnp.concatenate([q[a0 * 128 : a0 * 128 + 128, k * 128 : k * 128 + 128].T for k in range(2)], axis=1)
+                    for a0 in range(2)
+                ],
+                axis=0,
             )
-            for ri in range(2)
+            for q in e
         ]
-        th, tl = split(jnp.concatenate(across(x, right_hi[0], right_lo[0]), axis=0))
-        y = dot3((left_hi[1], left_lo[1]), (th, tl))
-        result[0, rows, wide] = y[:128]
-        result[1, rows, wide] = y[128:]
-        rh, rl = split(jnp.concatenate([rin[ri, rows, wide] for ri in range(2)], axis=0))
-        return acc + dot3((th, tl), (rh, rl), NT) + dot(tl, rl, NT)
-
-    return lax.fori_loop(0, 4, body, total)
+        t = across(x, right_hi[0], right_lo[0])
+        w = across([e[0], -e[1]], right_hi[0], right_lo[0])
+        for a0 in range(2):
+            rows = pl.ds(a0 * 128, 128)
+            th, tl = split(jnp.concatenate(halves(t, a0), axis=0))
+            y = dot3((left_hi[1], left_lo[1]), (th, tl))
+            result[0, rows, wide] = y[:128]
+            result[1, rows, wide] = y[128:]
+            r = [rin[ri, rows, wide] for ri in range(2)]
+            rh, rl = split(jnp.concatenate(r, axis=0))
+            first = first + dot3((th, tl), (rh, rl), NT) + dot(tl, rl, NT)
+            wh, wl = split(jnp.concatenate(halves(w, a0), axis=0))
+            r = [jnp.concatenate([q[:, k * 128 : k * 128 + 128] for q in r], axis=1) for k in range(2)]
+            rh, rl = split(jnp.concatenate(r, axis=0))
+            second = second + dot3((wh, wl), (rh, rl)) + dot(wl, rl)
+        return first, second
+
+    zero = jnp.zeros((256, 256), F32)
+    return lax.fori_loop(0, 4, body, (zero, zero))
+
+
+def upper_stage(upper, right_hi, right_lo, left_hi, left_lo, result, out, stored):
+    def body(i, carry):
+        wide = columns(i, 256)
+        t = across([upper[ri, :, wide] for ri in range(2)], right_hi[0], right_lo[0])
+        for a0 in range(2):
+            rows = pl.ds(a0 * 128, 128)
+            y = dot3((left_hi[1], left_lo[1]), split(jnp.concatenate(halves(t, a0), axis=0)))
+            result[0, rows, wide] += y[:128]
+            result[1, rows, wide] += y[128:]
+        pltpu.make_async_copy(result.at[:, :, wide], out.at[:, :, wide], stored.at[i]).start()
+        return carry
+
+    lax.fori_loop(0, 4, body, 0)
 
 
 def kernel(
     density, costate, phases, displacements, slots_hbm, checkpoint_hbm, out, grads,
-    result, cin, rin, work, turned, lower, disp, table, slots, checkpoint,
-    c_send0, c_send1, r_send0, r_send1, c_recv0, c_recv1, r_recv0, r_recv1, send_a, send_b, recv_a, recv_b,
-    t1, t2, t3, t4, g3, left_hi, left_lo, right_hi, right_lo, tile_ref, near, far,
+    result, cin, rin, work, turned, disp, table, slots, checkpoint,
+    c_send0, c_send1, r_send0, r_send1, recv_l, recv_u,
+    c_recv0, c_recv1, r_recv0, r_recv1, t1, t2, t3, t4, t5, t6, g3, left_hi, left_lo, right_hi, right_lo, tile_ref, near, far,
     ready, load, sem,
 ):
     c_send, r_send = (c_send0, c_send1), (r_send0, r_send1)
@@ -434,12 +464,12 @@
     pl.semaphore_wait(barrier, 30)
     for to in plane:
         pl.semaphore_signal(ready, inc=1, device_id=to, device_id_type=MESH)
+    c_sems = (sem.at[pl.ds(0, 2)], sem.at[pl.ds(2, 2)])
+    r_sems = (sem.at[pl.ds(4, 2)], sem.at[pl.ds(6, 2)])
+    send_near(0, c_send, c_recv, *c_sems, (for_first, lambda act: pl.semaphore_wait(ready, 15), for_rest))
     turn_over(cin, turned)
     pack(turned, c_send1, False)
-    pl.semaphore_wait(ready, 15)
-    c_sems = (sem.at[pl.ds(0, 2)], sem.at[pl.ds(2, 2)])
-    r_sems = (sem.at[pl.ds(4, 2)], sem.at[pl.ds(6, 2)])
-    send_near(c_send, c_recv, *c_sems)
+    send_near(1, c_send, c_recv, *c_sems, (for_others,))
 
     for copy in loads[4:]:
         copy.wait()
@@ -479,60 +509,66 @@
     loads[3].wait()
     rho_stage(rin, work, right_hi, right_lo, left_hi, left_lo)
     pack(work, r_send0, True)
+    send_near(0, r_send, r_recv, *r_sems, (for_others,))
     turn_over(work, turned)
     pack(turned, r_send1, True)
-    send_near(r_send, r_recv, *r_sems)
+    send_near(1, r_send, r_recv, *r_sems, (for_others,))
 
     wait_near(c_recv, c_sems[1])
     flip(c_recv1, t1, c_recv0)
     mode_one(t1, t2, g3, False)
     flip(t2, t1)
     mode_one(t1, t2, g3, True)
+    send_some(t2, recv_l, sem.at[8], sem.at[9], 0, 32)
     flip(t2, t3)
-    blend(t3, t2, send_a, send_b)
-    send_all(send_a, recv_a, sem.at[8], sem.at[9])
-    send_all(send_b, recv_b, sem.at[10], sem.at[11])
-
-    flip(c_recv0, t2, c_recv1, False)
-    mode_one(t2, t3, g3, True)
-    flip(t3, t2)
+
+    flip(c_recv0, t4, c_recv1, False)
+    mode_one(t4, t5, g3, True)
+    flip(t5, t4)
     wait_near(r_recv, r_sems[1])
-    flip(r_recv1, t3, r_recv0)
-    flip(t3, t4)
-    f = gram(t1, t4, 1.0) + gram(t2, t3, -1.0)
+    flip(r_recv1, t5, r_recv0)
+    flip(t5, t6)
+    f = gram(t1, t6, 1.0) + gram(t4, t5, -1.0)
     row0, row1 = diagonals(ua, va, wa, (f[:64], f[64:]))
 
-    total = jnp.zeros((256, 256), F32)
-    stores = []
-    for a0, (recv, number) in enumerate(((recv_a, 9), (recv_b, 11))):
-        wait_tiles(recv, sem.at[number], TILES - 1)
-        unpack(recv, work, lower)
-        total = final_stage(
-            work, lower, rin, right_hi, right_lo, left_hi, left_lo, result, pl.ds(a0 * 128, 128), total
-        )
-        for ri in range(2):
-            rows = pl.ds(a0 * 128, 128)
-            copy = pltpu.make_async_copy(result.at[ri, rows], out.at[ri, rows], load.at[a0 * 2 + ri])
-            copy.start()
-            stores.append(copy)
-    j = (total[:128, :128] + total[128:, 128:], total[128:, :128] - total[:128, 128:])
+    send_some(t3, recv_u, sem.at[10], sem.at[11], 0, 19)
+    wait_tiles(recv_l, sem.at[9], TILES - 1)
+    unpack(recv_l, work, True)
+    m, n = lower_stage(work, rin, right_hi, right_lo, left_hi, left_lo, result)
+    j = (
+        m[:128, :128] + m[128:, 128:] + n[:128, :128] - n[128:, 128:],
+        m[128:, :128] - m[:128, 128:] + n[:128, 128:] + n[128:, :128],
+    )
     row2, row3 = diagonals(ub, vb, wb, j)
     blank = jnp.zeros((1, 64), F32)
     tile_ref[0] = jnp.concatenate(
         [jnp.concatenate([row0, blank], axis=1), jnp.concatenate([row1, blank], axis=1), row2, row3,
          jnp.zeros((4, 128), F32)], axis=0)
 
-    for half, (group, held) in enumerate(((ring, near), (plane, far))):
+    def spread_out(half, group, held):
         for k, to in enumerate(group):
             pltpu.make_async_remote_copy(
                 src_ref=tile_ref.at[half], dst_ref=held.at[k], send_sem=sem.at[12 + half],
                 recv_sem=sem.at[14 + half], device_id=to, device_id_type=MESH,
             ).start()
+
+    def add_up(half, held):
         pltpu.make_async_copy(held, held, sem.at[14 + half]).wait()
         value = tile_ref[half]
         for k in range(15):
             value = value + held[k]
         tile_ref[half + 1] = value
+
+    spread_out(0, ring, near)
+    send_some(t3, recv_u, sem.at[10], sem.at[11], 19, 32)
+    add_up(0, near)
+    spread_out(1, plane, far)
+
+    wait_tiles(recv_u, sem.at[11], TILES - 1)
+    unpack(recv_u, work, False)
+    upper_stage(work, right_hi, right_lo, left_hi, left_lo, result, out, load)
+
+    add_up(1, far)
     summed = tile_ref[2]
     modes = dot(summed, spread, NN, HIGHEST)
     for layer in range(2):
@@ -542,10 +578,11 @@
         pltpu.make_async_copy(held, held, sem.at[12 + half]).wait()
     wait_near_sent(c_send, c_sems[0])
     wait_near_sent(r_send, r_sems[0])
-    wait_tiles(send_a, sem.at[8], TILES - 1)
-    wait_tiles(send_b, sem.at[10], TILES - 1)
-    for copy in stores:
-        copy.wait()
+    wait_tiles(t2, sem.at[8], TILES - 1)
+    wait_tiles(t3, sem.at[10], TILES - 1)
+    for k in range(4):
+        wide = pl.ds(k * 256, 256)
+        pltpu.make_async_copy(result.at[:, :, wide], out.at[:, :, wide], load.at[k]).wait()
 
 
 def per_device(density, costate, phases, displacements, table_slot, checkpoint):
@@ -562,13 +599,12 @@
         out_specs=(anywhere, vmem),
         scratch_shapes=[field] * 5
         + [
-            pltpu.VMEM((2, 128, 1024), F32),
             pltpu.VMEM(displacements.shape, F32),
             pltpu.VMEM(phases.shape, F32),
             pltpu.SMEM(table_slot.shape, jnp.int32),
             pltpu.SMEM(checkpoint.shape, jnp.int32),
         ]
-        + [tiles] * 4 + [spaced] * 4 + [tiles] * 4 + [spaced] * 4
+        + [tiles] * 6 + [spaced] * 10
         + [pltpu.VMEM((128, 192), BF16)]
         + [matrix] * 4
         + [
@@ -580,7 +616,7 @@
             pltpu.SemaphoreType.DMA((16,)),
         ],
         compiler_params=pltpu.CompilerParams(
-            collective_id=0, has_side_effects=True, vmem_limit_bytes=52 * 2**20
+            collective_id=0, has_side_effects=True, vmem_limit_bytes=50 * 2**20
         ),
     )(density, costate, phases, displacements, table_slot, checkpoint)
 

time: 118 us -> 112 us (0.949)
  Pallas kernels: 112 us -> 107 us
  local copies, waits for them, and re-layouts: 5.12 us -> 3.28 us
    pallas_call x1, Pallas kernels: 112 us -> 107 us  [per_device(): pl.pallas_call(kernel, out_shape=(jax.ShapeDtypeStruct(costate.shape, F32...]
    unnamed x6, local copies, waits for them, and re-layouts: 5.12 us -> 3.28 us
where the time goes in v4:
time: 112 us
  Pallas kernels  107 us (96%)
  local copies, waits for them, and re-layouts  3.28 us (3%)
  between operations  1.3 us (1%)
    pallas_call x1, Pallas kernels, per_device(): pl.pallas_call(kernel, out_shape=(jax.ShapeDtypeStruct(costate.shape, F32...  107 us
    unnamed x6, local copies, waits for them, and re-layouts  3.28 us

profile of v4, /device:TPU:1, one launch (start us, length us, event | category | flops | bytes accessed | tf_op | source)
XLA Modules:
  0.0 111.6 jit_solution(17333447457610427117)
XLA Ops:
  1.3 0.0 copy-start
  1.3 0.7 copy-done
  2.0 0.0 copy-start.1
  2.0 0.7 copy-done.1
  2.7 107.0 %shard_map.77 = (f32[2,256,1024]{2,1,0:T(8,128)S(1)}, f32[2,2,64]{2,1,0:T(2,128)S(1)}) custom-call(f32[2,256,1024]{2,1,0:T(8,128)} %density.1, f32[2,256,1024]{2,1,0:T(8,128)} %costate.1, f32[24,2,64]{2,1,0:T(2,128)S(1)} %copy-done, f32[24,2,2,64,64]{4,3,2,1,0:T(8,128)} %displacements.1, s32[24]{0:T(128)S(1)} %copy-done.1, s32[1]{0:T(128)S(6)} %copy.10.checkpoint_hbm), custom_call_target="tpu_custom_call" | custom-call | tf_op jit(solution)/shard_map/pallas_call | solution.py:595
  109.7 1.3 %copy.11 = f32[2,256,1024]{2,1,0:T(8,128)} copy(f32[2,256,1024]{2,1,0:T(8,128)S(1)} %get-tuple-element.4) | data formatting | bytes 4194304
  111.0 0.6 copy.12
Async XLA Ops:
  1.3 0.7 copy-start
  2.0 0.7 copy-start.1

commit v5 on v4

--- a/solution.py
+++ b/solution.py
@@ -338,8 +338,11 @@
     return lax.fori_loop(0, 8, body, jnp.zeros((128, 64), F32))
 
 
-def cmul(a, b, dims=NN):
+def cmul(a, b, dims=NN, exact=True):
     mul = functools.partial(dot, dims=dims, precision=HIGHEST)
+    if not exact:
+        a, b = [[split(q) for q in pair] for pair in (a, b)]
+        mul = functools.partial(dot3, dims=dims)
     return mul(a[0], b[0]) - mul(a[1], b[1]), mul(a[0], b[1]) + mul(a[1], b[0])
 
 
@@ -347,8 +350,8 @@
     return a[0], -a[1]
 
 
-def diagonals(u, v, w, m):
-    t = cmul(m, conj(v), NT)
+def diagonals(u, v, w, m, exact=True):
+    t = cmul(m, conj(v), NT, exact)
     first = jnp.sum(u[0] * m[1] - u[1] * m[0], axis=0, keepdims=True)
     second = jnp.sum(w[0] * t[1] - w[1] * t[0], axis=0, keepdims=True)
     return 2.0 * first, 2.0 * second
@@ -380,7 +383,7 @@
     return [q[a0 * 128 : a0 * 128 + 128] for q in x]
 
 
-def lower_stage(lower, rin, right_hi, right_lo, left_hi, left_lo, result):
+def lower_stage(lower, rin, right_hi, right_lo, across_lower):
     def body(i, acc):
         first, second = acc
         wide = columns(i, 256)
@@ -397,23 +400,36 @@
         ]
         t = across(x, right_hi[0], right_lo[0])
         w = across([e[0], -e[1]], right_hi[0], right_lo[0])
+        for ri in range(2):
+            across_lower[ri, :, wide] = t[ri]
         for a0 in range(2):
             rows = pl.ds(a0 * 128, 128)
             th, tl = split(jnp.concatenate(halves(t, a0), axis=0))
-            y = dot3((left_hi[1], left_lo[1]), (th, tl))
-            result[0, rows, wide] = y[:128]
-            result[1, rows, wide] = y[128:]
             r = [rin[ri, rows, wide] for ri in range(2)]
             rh, rl = split(jnp.concatenate(r, axis=0))
-            first = first + dot3((th, tl), (rh, rl), NT) + dot(tl, rl, NT)
+            first = first + dot3((th, tl), (rh, rl), NT)
             wh, wl = split(jnp.concatenate(halves(w, a0), axis=0))
             r = [jnp.concatenate([q[:, k * 128 : k * 128 + 128] for q in r], axis=1) for k in range(2)]
             rh, rl = split(jnp.concatenate(r, axis=0))
-            second = second + dot3((wh, wl), (rh, rl)) + dot(wl, rl)
+            second = second + dot3((wh, wl), (rh, rl))
         return first, second
 
     zero = jnp.zeros((256, 256), F32)
     return lax.fori_loop(0, 4, body, (zero, zero))
+
+
+def down_stage(across_lower, left_hi, left_lo, result):
+    def body(i, carry):
+        wide = columns(i, 256)
+        for a0 in range(2):
+            rows = pl.ds(a0 * 128, 128)
+            t = [across_lower[ri, rows, wide] for ri in range(2)]
+            y = dot3((left_hi[1], left_lo[1]), split(jnp.concatenate(t, axis=0)))
+            result[0, rows, wide] = y[:128]
+            result[1, rows, wide] = y[128:]
+        return carry
+
+    lax.fori_loop(0, 4, body, 0)
 
 
 def upper_stage(upper, right_hi, right_lo, left_hi, left_lo, result, out, stored):
@@ -528,18 +544,18 @@
     wait_near(r_recv, r_sems[1])
     flip(r_recv1, t5, r_recv0)
     flip(t5, t6)
+    send_some(t3, recv_u, sem.at[10], sem.at[11], 0, 19)
     f = gram(t1, t6, 1.0) + gram(t4, t5, -1.0)
     row0, row1 = diagonals(ua, va, wa, (f[:64], f[64:]))
 
-    send_some(t3, recv_u, sem.at[10], sem.at[11], 0, 19)
     wait_tiles(recv_l, sem.at[9], TILES - 1)
     unpack(recv_l, work, True)
-    m, n = lower_stage(work, rin, right_hi, right_lo, left_hi, left_lo, result)
+    m, n = lower_stage(work, rin, right_hi, right_lo, turned)
     j = (
         m[:128, :128] + m[128:, 128:] + n[:128, :128] - n[128:, 128:],
         m[128:, :128] - m[:128, 128:] + n[:128, 128:] + n[128:, :128],
     )
-    row2, row3 = diagonals(ub, vb, wb, j)
+    row2, row3 = diagonals(ub, vb, wb, j, False)
     blank = jnp.zeros((1, 64), F32)
     tile_ref[0] = jnp.concatenate(
         [jnp.concatenate([row0, blank], axis=1), jnp.concatenate([row1, blank], axis=1), row2, row3,
@@ -561,6 +577,7 @@
 
     spread_out(0, ring, near)
     send_some(t3, recv_u, sem.at[10], sem.at[11], 19, 32)
+    down_stage(turned, left_hi, left_lo, result)
     add_up(0, near)
     spread_out(1, plane, far)
 

time: 112 us -> 107 us (0.955)
  Pallas kernels: 107 us -> 102 us
    pallas_call x1, Pallas kernels: 107 us -> 102 us  [per_device(): pl.pallas_call(kernel, out_shape=(jax.ShapeDtypeStruct(costate.shape, F32...]
where the time goes in v5:
time: 107 us
  Pallas kernels  102 us (95%)
  local copies, waits for them, and re-layouts  3.28 us (3%)
  between operations  1.3 us (1%)
    pallas_call x1, Pallas kernels, per_device(): pl.pallas_call(kernel, out_shape=(jax.ShapeDtypeStruct(costate.shape, F32...  102 us
    unnamed x6, local copies, waits for them, and re-layouts  3.28 us

profile of v5, /device:TPU:1, one launch (start us, length us, event | category | flops | bytes accessed | tf_op | source)
XLA Modules:
  0.0 106.7 jit_solution(15334883757608072276)
XLA Ops:
  1.3 0.0 copy-start
  1.3 0.7 copy-done
  2.0 0.0 copy-start.1
  2.0 0.7 copy-done.1
  2.7 102.2 %shard_map.77 = (f32[2,256,1024]{2,1,0:T(8,128)S(1)}, f32[2,2,64]{2,1,0:T(2,128)S(1)}) custom-call(f32[2,256,1024]{2,1,0:T(8,128)} %density.1, f32[2,256,1024]{2,1,0:T(8,128)} %costate.1, f32[24,2,64]{2,1,0:T(2,128)S(1)} %copy-done, f32[24,2,2,64,64]{4,3,2,1,0:T(8,128)} %displacements.1, s32[24]{0:T(128)S(1)} %copy-done.1, s32[1]{0:T(128)S(6)} %copy.10.checkpoint_hbm), custom_call_target="tpu_custom_call" | custom-call | tf_op jit(solution)/shard_map/pallas_call | solution.py:612
  104.8 1.3 %copy.11 = f32[2,256,1024]{2,1,0:T(8,128)} copy(f32[2,256,1024]{2,1,0:T(8,128)S(1)} %get-tuple-element.4) | data formatting | bytes 4194304
  106.2 0.6 copy.12
Async XLA Ops:
  1.3 0.7 copy-start
  2.0 0.7 copy-start.1
